TPU v7x, 32 devices: a whole 2x2x4 slice. The times are simulated.
32 devices in a mesh: fsdp: 32 (over z, y, x, core).
Axes of the slice: x: 2, y: 2, z: 4, core: 2. Of those that a mesh axis runs over, the one named last changes fastest.
Arguments:
- tokens: bfloat16 [4096, 768], P('fsdp'), may hold values from -6 to 6
- cotangent: bfloat16 [4096, 768], P('fsdp'), may hold values from -6 to 6
- lengths: int32 [64], replicated, may hold values from 1 to 127, as said below
- owner: int32 [64], replicated, may hold values from 0 to 31, as said below
- offsets: int32 [64], replicated, may hold values from 0 to 127, as said below
- ln1_gain: bfloat16 [768], P('fsdp'), may hold values from 0.099609375 to 1.8984375
- ln1_bias: bfloat16 [768], P('fsdp'), may hold values from -1.796875 to 1.796875
- w_qkv: bfloat16 [768, 2304], P('fsdp'), may hold values from -0.21875 to 0.21875
- b_query: bfloat16 [768], P('fsdp'), may hold values from -1.796875 to 1.796875
- b_value: bfloat16 [768], P('fsdp'), may hold values from -1.796875 to 1.796875
- w_proj: bfloat16 [768, 768], P('fsdp'), may hold values from -0.625 to 0.625
- b_proj: bfloat16 [768], P('fsdp'), may hold values from -1.796875 to 1.796875
- ln2_gain: bfloat16 [768], P('fsdp'), may hold values from 0.099609375 to 1.8984375
- ln2_bias: bfloat16 [768], P('fsdp'), may hold values from -1.796875 to 1.796875
- w_fc: bfloat16 [768, 3072], P('fsdp'), may hold values from -0.21875 to 0.21875
- b_fc: bfloat16 [3072], P('fsdp'), may hold values from -1.796875 to 1.796875
- w_out: bfloat16 [3072, 768], P('fsdp'), may hold values from -0.21875 to 0.21875
- b_out: bfloat16 [768], P('fsdp'), may hold values from -1.796875 to 1.796875
Outputs:
- result: bfloat16 [4096, 768], P('fsdp')
- grad_tokens: bfloat16 [4096, 768], P('fsdp')
- grad_ln1_gain: float32 [768], P('fsdp')
- grad_ln1_bias: float32 [768], P('fsdp')
- grad_w_qkv: float32 [768, 2304], P('fsdp')
- grad_b_query: float32 [768], P('fsdp')
- grad_b_value: float32 [768], P('fsdp')
- grad_w_proj: float32 [768, 768], P('fsdp')
- grad_b_proj: float32 [768], P('fsdp')
- grad_ln2_gain: float32 [768], P('fsdp')
- grad_ln2_bias: float32 [768], P('fsdp')
- grad_w_fc: float32 [768, 3072], P('fsdp')
- grad_b_fc: float32 [3072], P('fsdp')
- grad_w_out: float32 [3072, 768], P('fsdp')
- grad_b_out: float32 [768], P('fsdp')
Inputs may be any that keep to these rules, and one draw needn't show every extreme that they name: Each device owns exactly two sequences, placed one after the other from slot 0 of its slots; their lengths add up to at most 128, and on some device to exactly 128. `owner`: every device owns exactly two sequences. `offsets`: A device's first sequence starts at slot 0, its second right after the first.
All inputs are finite; a program needn't handle non-finite values.
Results may differ from a plain program's by a relative error of at most 0.012.
Values may be sent and summed in bfloat16 or wider, within the bound.
A program may use at most 192 MiB of HBM per device.

v0:
```python
import math

import jax
import jax.numpy as jnp
from jax import lax
from jax.sharding import PartitionSpec as P

H = 12
HD = 64


gelu_scale = 0.7978845608028654


def norm_forward(values, gain, shift):
    center = values - jnp.mean(values, axis=-1, keepdims=True)
    inv_std = lax.rsqrt(jnp.mean(center * center, axis=-1, keepdims=True) + 1e-05)
    normal = center * inv_std
    return (normal * gain + shift, normal, inv_std)


def norm_backward(upstream, normal, inv_std, gain):
    grad_gain = jnp.sum(upstream * normal, axis=0)
    grad_shift = jnp.sum(upstream, axis=0)
    scaled = upstream * gain
    inner = (
        scaled
        - jnp.mean(scaled, axis=-1, keepdims=True)
        - normal * jnp.mean(scaled * normal, axis=-1, keepdims=True)
    )
    return (inner * inv_std, grad_gain, grad_shift)


def outer_sum(left, right):
    return lax.dot_general(
        left, right, (((0,), (0,)), ((), ())), preferred_element_type=jnp.float32
    )


def through(left, weight):
    return lax.dot_general(
        left, weight, (((1,), (1,)), ((), ())), preferred_element_type=jnp.float32
    )


def column_sum(values):
    return jnp.sum(values.astype(jnp.float32), axis=0)


def pack_rows(pieces, groups):
    return jnp.concatenate([piece.reshape(groups, -1) for piece in pieces], axis=1)


def unpack_rows(packed, layouts, groups):
    pieces = []
    begin_at = 0
    for layout in layouts:
        column_count = math.prod(layout) // groups
        pieces.append(packed[:, begin_at : begin_at + column_count].reshape(layout))
        begin_at = begin_at + column_count
    return tuple(pieces)


def body(
    tokens,
    cotangent,
    lengths,
    owner,
    offsets,
    ln1_gain,
    ln1_bias,
    w_qkv,
    b_query,
    b_value,
    w_proj,
    b_proj,
    ln2_gain,
    ln2_bias,
    w_fc,
    b_fc,
    w_out,
    b_out,
):
    slot_count, width = tokens.shape
    devices_all = lax.axis_size("fsdp")
    shards = (
        ln1_gain,
        ln1_bias,
        w_qkv,
        b_query,
        b_value,
        w_proj,
        b_proj,
        ln2_gain,
        ln2_bias,
        w_fc,
        b_fc,
        w_out,
        b_out,
    )
    shard_layouts = [piece.shape for piece in shards]
    whole_layouts = [(piece.shape[0] * devices_all,) + tuple(piece.shape[1:]) for piece in shards]
    packed_shards = pack_rows(shards, 1)
    gathered = lax.all_gather(packed_shards, "fsdp", axis=0, tiled=True)
    (
        gain_one,
        shift_one,
        w_joined,
        bias_query,
        bias_value,
        w_project,
        bias_project,
        gain_two,
        shift_two,
        w_hidden,
        bias_hidden,
        w_final,
        bias_final,
    ) = unpack_rows(gathered, whole_layouts, devices_all)
    device = lax.axis_index("fsdp")
    slots = jnp.arange(slot_count, dtype=jnp.int32)
    inside = (
        (owner[:, None] == device)
        & (offsets[:, None] <= slots[None, :])
        & (slots[None, :] < (offsets + lengths)[:, None])
    )
    numbers = jnp.arange(lengths.shape[0], dtype=jnp.int32)[:, None] + 1
    labels = jnp.sum(jnp.where(inside, numbers, 0), axis=0) - 1
    allowed = (labels[:, None] == labels[None, :]) & (slots[None, :] <= slots[:, None])
    valid = (labels >= 0).astype(jnp.float32)
    inputs = tokens.astype(jnp.float32)
    first_out, normal_one, inv_one = norm_forward(
        inputs, gain_one.astype(jnp.float32), shift_one.astype(jnp.float32)
    )
    normed = first_out.astype(jnp.bfloat16)
    joined = jnp.dot(normed, w_joined, preferred_element_type=jnp.float32)
    query = (
        (joined[:, :width] + bias_query.astype(jnp.float32))
        .astype(jnp.bfloat16)
        .reshape(slot_count, H, HD)
    )
    keys = joined[:, width : 2 * width].astype(jnp.bfloat16).reshape(slot_count, H, HD)
    values = (
        (joined[:, 2 * width :] + bias_value.astype(jnp.float32))
        .astype(jnp.bfloat16)
        .reshape(slot_count, H, HD)
    )
    scores = jnp.einsum("qhd,khd->hqk", query, keys, preferred_element_type=jnp.float32) * 0.125
    masked = jnp.where(allowed[None], scores, -1e30)
    row_top = jnp.max(masked, axis=-1, keepdims=True)
    expo = jnp.exp(masked - row_top)
    row_total = jnp.sum(expo, axis=-1, keepdims=True)
    probs = expo / row_total
    log_total = row_top + jnp.log(row_total)
    mixed = (
        jnp.einsum(
            "hqk,khd->qhd", probs.astype(jnp.bfloat16), values, preferred_element_type=jnp.float32
        )
        .reshape(slot_count, width)
        .astype(jnp.bfloat16)
    )
    middle = (
        inputs
        + jnp.dot(mixed, w_project, preferred_element_type=jnp.float32)
        + bias_project.astype(jnp.float32)
    )
    second_out, normal_two, inv_two = norm_forward(
        middle, gain_two.astype(jnp.float32), shift_two.astype(jnp.float32)
    )
    second = second_out.astype(jnp.bfloat16)
    hidden = jnp.dot(second, w_hidden, preferred_element_type=jnp.float32) + bias_hidden.astype(
        jnp.float32
    )
    tanh_part = jnp.tanh(gelu_scale * (hidden + 0.044715 * hidden * hidden * hidden))
    active = (0.5 * hidden * (1.0 + tanh_part)).astype(jnp.bfloat16)
    result = (
        middle
        + jnp.dot(active, w_final, preferred_element_type=jnp.float32)
        + bias_final.astype(jnp.float32)
    )
    regathered = lax.all_gather(packed_shards, "fsdp", axis=0, tiled=True)
    (
        gain_one,
        shift_one,
        w_joined,
        bias_query,
        bias_value,
        w_project,
        bias_project,
        gain_two,
        shift_two,
        w_hidden,
        bias_hidden,
        w_final,
        bias_final,
    ) = unpack_rows(regathered, whole_layouts, devices_all)
    grad_result = cotangent.astype(jnp.float32) * valid[:, None]
    grad_low = grad_result.astype(jnp.bfloat16)
    grad_bias_final = column_sum(grad_low)
    grad_w_final = outer_sum(active, grad_low)
    grad_active = through(grad_low, w_final)
    slope = 0.5 * (1.0 + tanh_part) + 0.5 * hidden * (1.0 - tanh_part * tanh_part) * gelu_scale * (
        1.0 + 3.0 * 0.044715 * hidden * hidden
    )
    grad_hidden = (grad_active * slope).astype(jnp.bfloat16)
    grad_bias_hidden = column_sum(grad_hidden)
    grad_w_hidden = outer_sum(second, grad_hidden)
    grad_second = through(grad_hidden, w_hidden)
    norm_grad_two, grad_gain_two, grad_shift_two = norm_backward(
        grad_second, normal_two, inv_two, gain_two.astype(jnp.float32)
    )
    grad_middle = grad_result + norm_grad_two
    grad_branch = grad_middle.astype(jnp.bfloat16)
    grad_bias_project = column_sum(grad_branch)
    grad_w_project = outer_sum(mixed, grad_branch)
    grad_mixed = through(grad_branch, w_project).astype(jnp.bfloat16).reshape(slot_count, H, HD)
    again = jnp.einsum("qhd,khd->hqk", query, keys, preferred_element_type=jnp.float32) * 0.125
    probs_again = jnp.exp(jnp.where(allowed[None], again, -1e30) - log_total)
    grad_probs = jnp.einsum("qhd,khd->hqk", grad_mixed, values, preferred_element_type=jnp.float32)
    grad_values = jnp.einsum(
        "hqk,qhd->khd",
        probs_again.astype(jnp.bfloat16),
        grad_mixed,
        preferred_element_type=jnp.float32,
    )
    row_inner = jnp.sum(grad_probs * probs_again, axis=-1, keepdims=True)
    grad_scores = (probs_again * (grad_probs - row_inner)).astype(jnp.bfloat16)
    grad_query = (
        jnp.einsum("hqk,khd->qhd", grad_scores, keys, preferred_element_type=jnp.float32) * 0.125
    )
    grad_keys = (
        jnp.einsum("hqk,qhd->khd", grad_scores, query, preferred_element_type=jnp.float32) * 0.125
    )
    grad_query = grad_query.astype(jnp.bfloat16).reshape(slot_count, width)
    grad_keys = grad_keys.astype(jnp.bfloat16).reshape(slot_count, width)
    grad_values = grad_values.astype(jnp.bfloat16).reshape(slot_count, width)
    grad_bias_query = column_sum(grad_query)
    grad_bias_value = column_sum(grad_values)
    grad_joined = jnp.concatenate([grad_query, grad_keys, grad_values], axis=1)
    grad_w_joined = outer_sum(normed, grad_joined)
    grad_normed = through(grad_joined, w_joined)
    norm_grad_one, grad_gain_one, grad_shift_one = norm_backward(
        grad_normed, normal_one, inv_one, gain_one.astype(jnp.float32)
    )
    grad_inputs = grad_middle + norm_grad_one
    every_packed = pack_rows(
        (
            grad_gain_one,
            grad_shift_one,
            grad_w_joined,
            grad_bias_query,
            grad_bias_value,
            grad_w_project,
            grad_bias_project,
            grad_gain_two,
            grad_shift_two,
            grad_w_hidden,
            grad_bias_hidden,
            grad_w_final,
            grad_bias_final,
        ),
        devices_all,
    )
    every_summed = lax.psum_scatter(every_packed, "fsdp", scatter_dimension=0, tiled=True)
    all_shards = unpack_rows(every_summed, shard_layouts, 1)
    return (
        result.astype(jnp.bfloat16),
        grad_inputs.astype(jnp.bfloat16),
        all_shards[0],
        all_shards[1],
        all_shards[2],
        all_shards[3],
        all_shards[4],
        all_shards[5],
        all_shards[6],
        all_shards[7],
        all_shards[8],
        all_shards[9],
        all_shards[10],
        all_shards[11],
        all_shards[12],
    )


def solution(mesh):
    in_specs = (
        P("fsdp", None),
        P("fsdp", None),
        P(),
        P(),
        P(),
        P("fsdp"),
        P("fsdp"),
        P("fsdp", None),
        P("fsdp"),
        P("fsdp"),
        P("fsdp", None),
        P("fsdp"),
        P("fsdp"),
        P("fsdp"),
        P("fsdp", None),
        P("fsdp"),
        P("fsdp", None),
        P("fsdp"),
    )
    out_specs = (
        P("fsdp", None),
        P("fsdp", None),
        P("fsdp"),
        P("fsdp"),
        P("fsdp", None),
        P("fsdp"),
        P("fsdp"),
        P("fsdp", None),
        P("fsdp"),
        P("fsdp"),
        P("fsdp"),
        P("fsdp", None),
        P("fsdp"),
        P("fsdp", None),
        P("fsdp"),
    )
    return jax.shard_map(body, mesh=mesh, in_specs=in_specs, out_specs=out_specs, check_vma=False)
```

profile of v0, /device:TPU:0, one launch (start us, length us, event | category | flops | bytes accessed | tf_op | source)
XLA Modules:
  0.0 872.9 jit_solution(12652017709351911691)
XLA Ops:
  13.3 3.3 dynamic-update-slice.15
  19.4 4.7 dynamic-update-slice.22
  24.3 4.6 dynamic-update-slice.24
  33.0 170.0 %all-gather.3.cloned.1.call-done = bf16[32,1,221472]{2,1,0:T(2,128)(2,1)} async-done(((bf16[1,1,221472]{2,1,0:T(2,128)(2,1)}), bf16[32,1,221472]{2,1,0:T(2,128)(2,1)}) %all-gather.3.cloned.1.call-update) | async-done | bytes 14174224 | tf_op jit(solution)/shard_map/all_gather | solution.py:104
  203.0 15.0 %copy.79 = bf16[32,1,221472]{2,0,1:T(8,128)(2,1)S(1)} copy(bf16[32,1,221472]{2,1,0:T(2,128)(2,1)} %all-gather.3.cloned.1.call-done) | data formatting | bytes 28348416
  219.9 3.2 copy-done
  224.4 9.9 %fusion.51 = (bf16[32,73728]{1,0:T(8,128)(2,1)}, bf16[32,73728]{1,0:T(8,128)(2,1)}) fusion(bf16[32,221472]{1,0:T(8,128)(2,1)} %bitcast.86), kind=kLoop, calls=%fused_computation.124 | loop fusion | bytes 18874368 | tf_op jit(solution)/shard_map/slice | solution.py:59
  236.4 3.1 reshape.388
  242.7 2.8 fusion.48
  249.2 6.1 reshape.394
  255.3 6.1 reshape.393
  262.5 3.3 convolution_add_fusion
  266.0 2.4 convert_reduce_fusion
  268.5 2.3 multiply_reduce_fusion.1
  276.8 2.1 fusion.27
  278.9 4.1 fusion.34
  283.0 1.9 fusion.41
  285.0 5.2 fusion.50
  290.1 5.2 fusion.44
  295.5 6.6 reshape.401
  302.3 2.1 reshape.404
  304.7 8.2 reshape.408
  312.9 8.2 reshape.410
  324.1 20.5 %dynamic-update-slice.2 = f32[32,221472]{1,0:T(8,128)} dynamic-update-slice(f32[32,221472]{1,0:T(8,128)} %dynamic-update-slice.1, f32[32,55296]{1,0:T(8,128)} %reshape.401, s32[]{} %constant.65, s32[]{} %constant.67) | dynamic-update-slice | bytes 14155780
  347.6 8.9 %dynamic-update-slice.5 = f32[32,221472]{1,0:T(8,128)} dynamic-update-slice(f32[32,221472]{1,0:T(8,128)} %dynamic-update-slice.4, f32[32,18432]{1,0:T(8,128)S(1)} %reshape.404, s32[]{} %constant.65, s32[]{} %constant.70) | dynamic-update-slice | bytes 4718596
  359.5 1.5 dynamic-update-slice.8
  361.0 28.8 %dynamic-update-slice.9 = f32[32,221472]{1,0:T(8,128)} dynamic-update-slice(f32[32,221472]{1,0:T(8,128)} %dynamic-update-slice.8, f32[32,73728]{1,0:T(8,128)} %reshape.408, s32[]{} %constant.65, s32[]{} %constant.74) | dynamic-update-slice | bytes 18874372
  391.3 28.3 %dynamic-update-slice.11 = f32[32,221472]{1,0:T(8,128)} dynamic-update-slice(f32[32,221472]{1,0:T(8,128)} %dynamic-update-slice.10, f32[32,73728]{1,0:T(8,128)} %reshape.410, s32[]{} %constant.65, s32[]{} %constant.76) | dynamic-update-slice | bytes 18874372
  423.1 4.7 fusion.9
  427.9 425.0 %all-reduce.3.cloned.1.call-done = f32[32,221472]{1,0:T(8,128)} async-done(((f32[32,221472]{1,0:T(8,128)}), f32[32,221472]{1,0:T(8,128)}) %all-reduce.3.cloned.1.call-update) | async-done | bytes 28348432
  852.8 2.2 dynamic-slice_reduce_fusion.2
  857.7 4.1 dynamic-slice_reduce_fusion
  (214 shorter events, 53.4 us)
Async XLA Ops:
  7.2 9.4 %copy-start.48 = (bf16[24]{0:T(256)(128)(2,1)S(1)}, bf16[24]{0:T(256)(128)(2,1)}, u32[]{:S(2)}) copy-start(bf16[24]{0:T(256)(128)(2,1)} %param.26) | copy-start | bytes 148
  7.2 9.7 %copy-start.49 = (bf16[24]{0:T(256)(128)(2,1)S(1)}, bf16[24]{0:T(256)(128)(2,1)}, u32[]{:S(2)}) copy-start(bf16[24]{0:T(256)(128)(2,1)} %param.27) | copy-start | bytes 148
  7.2 11.4 %copy-start.50 = (bf16[24]{0:T(256)(128)(2,1)S(1)}, bf16[24]{0:T(256)(128)(2,1)}, u32[]{:S(2)}) copy-start(bf16[24]{0:T(256)(128)(2,1)} %param.29) | copy-start | bytes 148
  7.2 11.6 %copy-start.51 = (bf16[24]{0:T(256)(128)(2,1)S(1)}, bf16[24]{0:T(256)(128)(2,1)}, u32[]{:S(2)}) copy-start(bf16[24]{0:T(256)(128)(2,1)} %param.30) | copy-start | bytes 148
  7.2 11.9 %copy-start.52 = (bf16[24]{0:T(256)(128)(2,1)S(1)}, bf16[24]{0:T(256)(128)(2,1)}, u32[]{:S(2)}) copy-start(bf16[24]{0:T(256)(128)(2,1)} %param.31) | copy-start | bytes 148
  7.2 16.8 %copy-start.53 = (bf16[96]{0:T(256)(128)(2,1)S(1)}, bf16[96]{0:T(256)(128)(2,1)}, u32[]{:S(2)}) copy-start(bf16[96]{0:T(256)(128)(2,1)} %param.33) | copy-start | bytes 580
  7.2 195.7 %all-gather.3.cloned.1.call-start = ((), (), s32[]{:S(2)}) async-start(), calls=%async_computation | async-start | bytes 29246976 | tf_op jit(solution)/shard_map/all_gather | solution.py:104
  7.3 21.6 %copy-start.54 = (bf16[24]{0:T(256)(128)(2,1)S(1)}, bf16[24]{0:T(256)(128)(2,1)}, u32[]{:S(2)}) copy-start(bf16[24]{0:T(256)(128)(2,1)} %param.35) | copy-start | bytes 148
  10.4 20.1 %copy-start.55 = (s32[64]{0:T(128)S(1)}, s32[64]{0:T(128)}, u32[]{:S(2)}) copy-start(s32[64]{0:T(128)} %param.22) | copy-start | bytes 772
  10.4 20.1 %copy-start.56 = (s32[64]{0:T(128)S(1)}, s32[64]{0:T(128)}, u32[]{:S(2)}) copy-start(s32[64]{0:T(128)} %param.20) | copy-start | bytes 772
  10.4 20.1 %copy-start.57 = (s32[64]{0:T(128)S(1)}, s32[64]{0:T(128)}, u32[]{:S(2)}) copy-start(s32[64]{0:T(128)} %param.21) | copy-start | bytes 772
  10.4 20.2 %copy-start.5 = (bf16[128,768]{1,0:T(8,128)(2,1)S(1)}, bf16[128,768]{1,0:T(8,128)(2,1)}, u32[]{:S(2)}) copy-start(bf16[128,768]{1,0:T(8,128)(2,1)} %param.18) | copy-start | bytes 589828
  30.2 822.6 %all-reduce.3.cloned.1.call-start = ((), (), s32[]{:S(2)}) async-start(), calls=%async_computation.1 | async-start | bytes 56721408
  218.0 5.0 copy-start
  236.4 6.3 copy-start.40
  255.3 6.2 copy-start.29
  255.3 6.2 copy-start.28
  255.3 6.3 copy-start.27
  255.3 6.4 copy-start.6
  255.3 6.4 copy-start.20
  255.3 6.4 copy-start.36
  261.8 4.1 copy-start.46
  262.3 8.6 copy-start.30
  262.3 3.8 copy-start.10
  262.3 3.8 copy-start.19
  262.5 8.4 copy-start.37
  262.5 6.0 slice-start
  271.7 11.3 %copy-start.8 = (f32[128,768]{1,0:T(8,128)}, f32[128,768]{1,0:T(8,128)S(1)}, u32[]{:S(2)}) copy-start(f32[128,768]{1,0:T(8,128)S(1)} %get-tuple-element.26) | copy-start | bytes 1179652
  284.9 5.2 copy-start.3
  284.9 5.2 copy-start.47
  304.7 8.2 copy-start.43
  312.9 8.2 copy-start.33
  (30 other events, 50.6 us)
Sparse Core Ops, SparseCore 0:
  30.3 172.6 all-gather.2
  421.2 431.5 all-reduce.2
where the time goes:
time: 877 us; the launch traced here: 873 us
  waiting for transfers between devices  595 us (68%)
  local copies, waits for them, and re-layouts  216 us (25%)
  matrix products  39.4 us (4%)
  between operations  15 us (2%)
    unnamed x3, waiting for transfers between devices  425 us
    all_gather x1, waiting for transfers between devices, body(): gathered = lax.all_gather(packed_shards, 'fsdp', axis=0, tiled=True)  170 us
    unnamed x149, local copies, waits for them, and re-layouts  142 us
    reshape x13, local copies, waits for them, and re-layouts, pack_rows(): piece.reshape(groups, -1)  25.8 us
    reshape x10, local copies, waits for them, and re-layouts, unpack_rows(): pieces.append(packed[:, begin_at:begin_at + column_count].reshape(layout))  21.5 us
    slice x6, local copies, waits for them, and re-layouts, unpack_rows(): pieces.append(packed[:, begin_at:begin_at + column_count].reshape(layout))  19.8 us
  transfers between devices with their start and end apart: 2, of which 2 were waited for; matrix products, arithmetic and copies ran while one was open for 1% of the time, Pallas kernels for 0%

commit v1 on v0

--- a/solution.py
+++ b/solution.py
@@ -1,8 +1,8 @@
-import math
-
 import jax
 import jax.numpy as jnp
 from jax import lax
+from jax.experimental import pallas as pl
+from jax.experimental.pallas import tpu as pltpu
 from jax.sharding import PartitionSpec as P
 
 H = 12
@@ -47,18 +47,373 @@
     return jnp.sum(values.astype(jnp.float32), axis=0)
 
 
-def pack_rows(pieces, groups):
-    return jnp.concatenate([piece.reshape(groups, -1) for piece in pieces], axis=1)
-
-
-def unpack_rows(packed, layouts, groups):
-    pieces = []
-    begin_at = 0
-    for layout in layouts:
-        column_count = math.prod(layout) // groups
-        pieces.append(packed[:, begin_at : begin_at + column_count].reshape(layout))
-        begin_at = begin_at + column_count
-    return tuple(pieces)
+MESH = pl.DeviceIdType.MESH
+SMALL_ROWS = 16
+LANES = 128
+
+PIECES = (
+    (0, 0, None, 0),
+    (1, 0, None, 0),
+    (3, 0, 2, 0),
+    (4, 0, None, 0),
+    (2, 0, None, 1),
+    (3, 1, 2, 1),
+)
+
+
+def place(device):
+    return (device // 8, (device // 4) % 2, (device // 2) % 2, device % 2)
+
+
+def moved(device, zm, fy, fx, fc):
+    z, y, x, c = place(device)
+    z_new = ((z // 2 + zm // 2) % 2) * 2 + (z + zm) % 2
+    return z_new * 8 + ((y + fy) % 2) * 4 + ((x + fx) % 2) * 2 + (c + fc) % 2
+
+
+def mask_of(order, zm, second, third, core):
+    fy, fx = (second, third) if order == 0 else (third, second)
+    return (zm, fy, fx, core)
+
+
+def code(mask):
+    zm, fy, fx, fc = mask
+    return zm * 8 + fy * 4 + fx * 2 + fc
+
+
+def view(ref, lead, piece):
+    _, part, parts, _ = piece
+    if parts is None:
+        return ref.at[lead] if lead is not None else ref
+    rows = ref.shape[-2] // parts
+    if lead is None:
+        return ref.at[pl.ds(part * rows, rows)]
+    return ref.at[lead, pl.ds(part * rows, rows)]
+
+
+def greet(device):
+    barrier = pltpu.get_barrier_semaphore()
+    peers = [(1, 0, 0, 0), (2, 0, 0, 0), (3, 0, 0, 0), (0, 1, 0, 0), (0, 0, 1, 0), (0, 0, 0, 1)]
+    for peer in peers:
+        pl.semaphore_signal(
+            barrier, inc=1, device_id=(moved(device, *peer),), device_id_type=MESH
+        )
+    pl.semaphore_wait(barrier, len(peers))
+
+
+def gather_kernel(*refs):
+    shards, wholes = refs[:5], refs[5:10]
+    send_sem, recv_sem, own_sem = refs[10:]
+    device = lax.axis_index("fsdp")
+    greet(device)
+
+    def send(number, held, step):
+        piece = PIECES[number]
+        whole = wholes[piece[0]]
+        origin = moved(device, *held)
+        slot = code(held) + code(step)
+        mine = isinstance(held[0], int) and held == (0, 0, 0, 0)
+        source = view(shards[piece[0]], None, piece) if mine else view(whole, origin, piece)
+        return pltpu.make_async_remote_copy(
+            src_ref=source,
+            dst_ref=view(whole, origin, piece),
+            send_sem=send_sem.at[number, slot],
+            recv_sem=recv_sem.at[number, slot],
+            device_id=(moved(device, *step),),
+            device_id_type=MESH,
+        )
+
+    def arrived(number, mask):
+        piece = PIECES[number]
+        target = view(wholes[piece[0]], moved(device, *mask), piece)
+        return pltpu.make_async_remote_copy(
+            src_ref=target,
+            dst_ref=target,
+            send_sem=send_sem.at[number, code(mask)],
+            recv_sem=recv_sem.at[number, code(mask)],
+            device_id=(moved(device, 0, 0, 0, 1),),
+            device_id_type=MESH,
+        )
+
+    own = [
+        pltpu.make_async_copy(shards[k], wholes[k].at[device], own_sem.at[k]) for k in range(5)
+    ]
+    home = (0, 0, 0, 0)
+    pieces = range(len(PIECES))
+    for step in (3, 1, 2):
+        for n in pieces:
+            send(n, home, (step, 0, 0, 0)).start()
+    for n in pieces:
+        order = PIECES[n][3]
+        send(n, home, mask_of(order, 0, 1, 0, 0)).start()
+        send(n, home, mask_of(order, 0, 0, 1, 0)).start()
+        send(n, home, (0, 0, 0, 1)).start()
+    for copy in own:
+        copy.start()
+
+    def second(zm):
+        for n in pieces:
+            order = PIECES[n][3]
+            held = mask_of(order, zm, 1, 0, 0)
+            arrived(n, held).wait_recv()
+            send(n, held, mask_of(order, 0, 0, 1, 0)).start()
+            send(n, held, (0, 0, 0, 1)).start()
+
+    def along(zm):
+        for n in pieces:
+            order = PIECES[n][3]
+            held = (zm, 0, 0, 0)
+            arrived(n, held).wait_recv()
+            send(n, held, mask_of(order, 0, 1, 0, 0)).start()
+            send(n, held, mask_of(order, 0, 0, 1, 0)).start()
+            send(n, held, (0, 0, 0, 1)).start()
+
+    def third(k):
+        for n in pieces:
+            held = mask_of(PIECES[n][3], k % 4, k // 4, 1, 0)
+            arrived(n, held).wait_recv()
+            send(n, held, (0, 0, 0, 1)).start()
+
+    @pl.loop(1, 4)
+    def _(zm):
+        along(zm)
+
+    @pl.loop(0, 4)
+    def _(zm):
+        second(zm)
+
+    @pl.loop(0, 8)
+    def _(k):
+        third(k)
+
+    @pl.loop(0, 16)
+    def _(k):
+        for n in pieces:
+            arrived(n, (k // 4, (k // 2) % 2, k % 2, 1)).wait_recv()
+
+    for copy in own:
+        copy.wait()
+
+    @pl.loop(1, 32)
+    def _(k):
+        for n in pieces:
+            arrived(n, (k // 8, (k // 4) % 2, (k // 2) % 2, k % 2)).wait_send()
+
+
+def gather_all(shards, devices_all):
+    return pl.pallas_call(
+        gather_kernel,
+        out_shape=[
+            jax.ShapeDtypeStruct((devices_all,) + piece.shape, piece.dtype) for piece in shards
+        ],
+        in_specs=[pl.BlockSpec(memory_space=pl.ANY)] * 5,
+        out_specs=[pl.BlockSpec(memory_space=pl.ANY)] * 5,
+        scratch_shapes=[
+            pltpu.SemaphoreType.DMA((len(PIECES), 32)),
+            pltpu.SemaphoreType.DMA((len(PIECES), 32)),
+            pltpu.SemaphoreType.DMA((5,)),
+        ],
+        compiler_params=pltpu.CompilerParams(collective_id=0, has_side_effects=True),
+    )(*shards)
+
+
+def scatter_kernel(*refs):
+    grads, sums = refs[:5], refs[5:10]
+    helds, comes = refs[10:15], refs[15:20]
+    send_sem, recv_sem, load_sem = refs[20:]
+    device = lax.axis_index("fsdp")
+    pieces = range(len(PIECES))
+    sibling = (0, 0, 0, 1)
+
+    def load(n, mask):
+        piece = PIECES[n]
+        slot = code(mask) // 2
+        return pltpu.make_async_copy(
+            view(grads[piece[0]], moved(device, *mask), piece),
+            view(helds[piece[0]], slot, piece),
+            load_sem.at[n, slot],
+        )
+
+    def push(n, mask, step, source):
+        piece = PIECES[n]
+        slot = code(mask)
+        return pltpu.make_async_remote_copy(
+            src_ref=source,
+            dst_ref=view(comes[piece[0]], slot, piece),
+            send_sem=send_sem.at[n, slot],
+            recv_sem=recv_sem.at[n, slot],
+            device_id=(moved(device, *step),),
+            device_id_type=MESH,
+        )
+
+    def across(n, mask):
+        piece = PIECES[n]
+        other = mask[:3] + (1,)
+        return push(n, other, sibling, view(grads[piece[0]], moved(device, *other), piece))
+
+    def onward(n, mask, step):
+        piece = PIECES[n]
+        return push(n, mask, step, view(helds[piece[0]], code(mask) // 2, piece))
+
+    def total(n, mask, froms, target=None):
+        piece = PIECES[n]
+        slot = code(mask) // 2
+        load(n, mask).wait()
+        for other in froms:
+            into = view(comes[piece[0]], code(other), piece)
+            push(n, other, sibling, into).wait_recv()
+        held = view(helds[piece[0]], slot, piece)
+        result = held if target is None else view(sums[piece[0]], None, piece)
+        terms = [held] + [view(comes[piece[0]], code(other), piece) for other in froms]
+        rows, columns = held.shape
+        width = min(columns, 768)
+        for begin in range(0, columns, width):
+            value = terms[0][:, begin : begin + width].astype(jnp.float32)
+            for term in terms[1:]:
+                value = value + term[:, begin : begin + width].astype(jnp.float32)
+            result[:, begin : begin + width] = value.astype(result.dtype)
+
+    def loads(third, k):
+        for n in pieces:
+            mask = mask_of(PIECES[n][3], k % 4, 1 - k // 4, third, 0)
+            load(n, mask).start()
+
+    def sends(third, k):
+        for n in pieces:
+            mask = mask_of(PIECES[n][3], k % 4, 1 - k // 4, third, 0)
+            across(n, mask).start()
+
+    @pl.loop(0, 8)
+    def _(k):
+        loads(1, k)
+
+    greet(device)
+
+    @pl.loop(0, 8)
+    def _(k):
+        sends(1, k)
+
+    @pl.loop(0, 8)
+    def _(k):
+        loads(0, k)
+        sends(0, k)
+
+    @pl.loop(0, 8)
+    def _(k):
+        for n in pieces:
+            order = PIECES[n][3]
+            mask = mask_of(order, k % 4, 1 - k // 4, 1, 0)
+            total(n, mask, [mask[:3] + (1,)])
+            onward(n, mask, mask_of(order, 0, 0, 1, 0)).start()
+
+    @pl.loop(0, 4)
+    def _(zm):
+        for n in pieces:
+            order = PIECES[n][3]
+            mask = mask_of(order, zm, 1, 0, 0)
+            total(n, mask, [mask[:3] + (1,), mask_of(order, zm, 1, 1, 0)])
+            onward(n, mask, mask_of(order, 0, 1, 0, 0)).start()
+
+    @pl.loop(1, 4)
+    def _(zm):
+        for n in pieces:
+            order = PIECES[n][3]
+            mask = (zm, 0, 0, 0)
+            total(
+                n,
+                mask,
+                [(zm, 0, 0, 1), mask_of(order, zm, 0, 1, 0), mask_of(order, zm, 1, 0, 0)],
+            )
+            onward(n, mask, mask).start()
+
+    for n in pieces:
+        order = PIECES[n][3]
+        total(
+            n,
+            (0, 0, 0, 0),
+            [(0, 0, 0, 1), mask_of(order, 0, 0, 1, 0), mask_of(order, 0, 1, 0, 0)]
+            + [(zm, 0, 0, 0) for zm in (1, 2, 3)],
+            True,
+        )
+
+    @pl.loop(1, 32)
+    def _(k):
+        for n in pieces:
+            into = view(comes[PIECES[n][0]], k, PIECES[n])
+            push(n, (k // 8, (k // 4) % 2, (k // 2) % 2, k % 2), sibling, into).wait_send()
+
+
+def scatter_all(grads):
+    count = grads[0].shape[0]
+    return pl.pallas_call(
+        scatter_kernel,
+        out_shape=[jax.ShapeDtypeStruct(piece.shape[1:], jnp.float32) for piece in grads],
+        in_specs=[pl.BlockSpec(memory_space=pl.ANY)] * 5,
+        out_specs=[pl.BlockSpec(memory_space=pltpu.VMEM)] * 5,
+        scratch_shapes=[
+            pltpu.VMEM((count // 2,) + piece.shape[1:], piece.dtype) for piece in grads
+        ]
+        + [pltpu.VMEM(piece.shape, piece.dtype) for piece in grads]
+        + [
+            pltpu.SemaphoreType.DMA((len(PIECES), 32)),
+            pltpu.SemaphoreType.DMA((len(PIECES), 32)),
+            pltpu.SemaphoreType.DMA((len(PIECES), 16)),
+        ],
+        compiler_params=pltpu.CompilerParams(
+            collective_id=1, has_side_effects=True, vmem_limit_bytes=48 * 1024 * 1024
+        ),
+    )(*grads)
+
+
+def pack_small(vectors, rows):
+    table = jnp.concatenate([v.reshape(-1, rows) for v in vectors], axis=0)
+    return jnp.pad(table, ((0, SMALL_ROWS - table.shape[0]), (0, LANES - rows)))
+
+
+def gather_params(shards, devices_all):
+    vectors = tuple(shards[k] for k in (0, 1, 3, 4, 6, 7, 8, 12, 10))
+    matrices = tuple(shards[k] for k in (2, 5, 9, 11))
+    rows = vectors[0].shape[0]
+    if kernels_fit(devices_all, rows):
+        small = pack_small(vectors, rows)
+        *full, table = gather_all(matrices + (small,), devices_all)
+        full = [piece.reshape((-1,) + piece.shape[2:]) for piece in full]
+        ratio = vectors[-1].shape[0] // rows
+        table = table[:, : 8 + ratio, :rows].transpose(1, 0, 2)
+        small_full = [table[k].reshape(-1) for k in range(8)]
+        small_full.append(table[8:].transpose(1, 0, 2).reshape(-1))
+    else:
+        full = [lax.all_gather(piece, "fsdp", axis=0, tiled=True) for piece in matrices]
+        table = lax.all_gather(jnp.concatenate(vectors)[None], "fsdp", axis=0, tiled=True)
+        small_full = []
+        begin = 0
+        for piece in vectors:
+            small_full.append(table[:, begin : begin + piece.shape[0]].reshape(-1))
+            begin += piece.shape[0]
+    return full, small_full
+
+
+def scatter_grads(matrices, vectors, devices_all):
+    rows = vectors[0].shape[0] // devices_all
+    if kernels_fit(devices_all, rows):
+        table = [v.reshape(devices_all, -1, rows) for v in vectors]
+        table = jnp.concatenate(table, axis=1)
+        table = jnp.pad(table, ((0, 0), (0, SMALL_ROWS - table.shape[1]), (0, LANES - rows)))
+        blocks = [g.astype(jnp.bfloat16).reshape(devices_all, -1, g.shape[1]) for g in matrices]
+        *full, table = scatter_all(blocks + [table])
+        small = [table[k, :rows] for k in range(8)]
+        ratio = vectors[-1].shape[0] // vectors[0].shape[0]
+        small.append(table[8 : 8 + ratio, :rows].reshape(-1))
+        return full, small
+
+    def summed(piece):
+        return lax.psum_scatter(piece, "fsdp", scatter_dimension=0, tiled=True)
+
+    return [summed(piece) for piece in matrices], [summed(piece) for piece in vectors]
+
+
+def kernels_fit(devices_all, rows):
+    return devices_all == 32 and rows % 8 == 0 and rows <= LANES
 
 
 def body(
@@ -98,25 +453,17 @@
         w_out,
         b_out,
     )
-    shard_layouts = [piece.shape for piece in shards]
-    whole_layouts = [(piece.shape[0] * devices_all,) + tuple(piece.shape[1:]) for piece in shards]
-    packed_shards = pack_rows(shards, 1)
-    gathered = lax.all_gather(packed_shards, "fsdp", axis=0, tiled=True)
-    (
+    (w_joined, w_project, w_hidden, w_final), (
         gain_one,
         shift_one,
-        w_joined,
         bias_query,
         bias_value,
-        w_project,
         bias_project,
         gain_two,
         shift_two,
-        w_hidden,
+        bias_final,
         bias_hidden,
-        w_final,
-        bias_final,
-    ) = unpack_rows(gathered, whole_layouts, devices_all)
+    ) = gather_params(shards, devices_all)
     device = lax.axis_index("fsdp")
     slots = jnp.arange(slot_count, dtype=jnp.int32)
     inside = (
@@ -178,22 +525,6 @@
         + jnp.dot(active, w_final, preferred_element_type=jnp.float32)
         + bias_final.astype(jnp.float32)
     )
-    regathered = lax.all_gather(packed_shards, "fsdp", axis=0, tiled=True)
-    (
-        gain_one,
-        shift_one,
-        w_joined,
-        bias_query,
-        bias_value,
-        w_project,
-        bias_project,
-        gain_two,
-        shift_two,
-        w_hidden,
-        bias_hidden,
-        w_final,
-        bias_final,
-    ) = unpack_rows(regathered, whole_layouts, devices_all)
     grad_result = cotangent.astype(jnp.float32) * valid[:, None]
     grad_low = grad_result.astype(jnp.bfloat16)
     grad_bias_final = column_sum(grad_low)
@@ -243,42 +574,37 @@
         grad_normed, normal_one, inv_one, gain_one.astype(jnp.float32)
     )
     grad_inputs = grad_middle + norm_grad_one
-    every_packed = pack_rows(
+    full, small = scatter_grads(
+        (grad_w_joined, grad_w_project, grad_w_hidden, grad_w_final),
         (
             grad_gain_one,
             grad_shift_one,
-            grad_w_joined,
             grad_bias_query,
             grad_bias_value,
-            grad_w_project,
             grad_bias_project,
             grad_gain_two,
             grad_shift_two,
-            grad_w_hidden,
+            grad_bias_final,
             grad_bias_hidden,
-            grad_w_final,
-            grad_bias_final,
         ),
         devices_all,
     )
-    every_summed = lax.psum_scatter(every_packed, "fsdp", scatter_dimension=0, tiled=True)
-    all_shards = unpack_rows(every_summed, shard_layouts, 1)
     return (
         result.astype(jnp.bfloat16),
         grad_inputs.astype(jnp.bfloat16),
-        all_shards[0],
-        all_shards[1],
-        all_shards[2],
-        all_shards[3],
-        all_shards[4],
-        all_shards[5],
-        all_shards[6],
-        all_shards[7],
-        all_shards[8],
-        all_shards[9],
-        all_shards[10],
-        all_shards[11],
-        all_shards[12],
+        small[0],
+        small[1],
+        full[0],
+        small[2],
+        small[3],
+        full[1],
+        small[4],
+        small[5],
+        small[6],
+        full[2],
+        small[8],
+        full[3],
+        small[7],
     )
 
 

time: 877 us -> 258 us (0.29)
  the two profiles are of different devices: /device:TPU:0 before, /device:TPU:9 now
where the time goes in v1:
time: 258 us; the launch traced here: 257 us
  Pallas kernels  188 us (73%)
  matrix products  36 us (14%)
  local copies, waits for them, and re-layouts  24.1 us (9%)
  other arithmetic  7.65 us (3%)
    pallas_call x1, Pallas kernels, scatter_all(): pl.pallas_call(scatter_kernel, out_shape=[jax.ShapeDtypeStruct(piece.shap...  114 us
    pallas_call x1, Pallas kernels, gather_all(): pl.pallas_call(gather_kernel, out_shape=[jax.ShapeDtypeStruct((devices_al...  74.3 us
    dot_general x4, matrix products, outer_sum(): lax.dot_general(left, right, (((0,), (0,)), ((), ())), preferred_element_...  11.3 us
    reshape x9, local copies, waits for them, and re-layouts, scatter_grads(): table = [v.reshape(devices_all, -1, rows) for v in vectors]  10.6 us
    dot_general x4, matrix products, through(): lax.dot_general(left, weight, (((1,), (1,)), ((), ())), preferred_element...  7.99 us

profile of v1, /device:TPU:9, one launch (start us, length us, event | category | flops | bytes accessed | tf_op | source)
XLA Modules:
  0.0 256.9 jit_solution(3189001857116535218)
XLA Ops:
  2.0 1.0 convert_reduce_fusion.1
  3.1 1.1 fusion.28
  5.8 0.8 concatenate.9
  7.3 74.3 %shard_map.289 = (bf16[32,24,2304]{2,1,0:T(8,128)(2,1)}, bf16[32,24,768]{2,1,0:T(8,128)(2,1)}, bf16[32,24,3072]{2,1,0:T(8,128)(2,1)}, bf16[32,96,768]{2,1,0:T(8,128)(2,1)}, bf16[32,16,128]{2,1,0:T(8,128)(2,1)}) custom-call(bf16[24,2304]{1,0:T(8,128)(2,1)} %refs_0_.1, bf16[24,768]{1,0:T(8,128)(2,1)} %refs_1_.1, bf16[24,3072]{1,0:T(8,128)(2,1)} %refs_2_.1, ...), custom_call_target="tpu_custom_call" | custom-call | tf_op jit(solution)/shard_map/pallas_call | solution.py:204
  81.6 0.9 slice_bitcast_fusion
  83.7 2.7 %fusion.53 = f32[128,2304]{1,0:T(8,128)S(1)} fusion(bf16[768,2304]{1,0:T(8,128)(2,1)} %bitcast.94, bf16[128,768]{1,0:T(8,128)(2,1)S(1)} %copy-done, f32[768]{0:T(1024)S(1)} %reshape.348, f32[768]{0:T(1024)S(1)} %reshape.347, f32[128]{0:T(128)S(1)} %add_rsqrt_fusion.1, f32[128]{0:T(128)S(1)} %broadcast_multiply_fusion.5), kind=kOutput, calls=%fused_computation.126 | convolution fusion | flops 453574656 | bytes 4922368 | tf_op jit(solution)/shard_map/dot_general | solution.py:483
  88.4 1.0 copy-done.1
  90.2 3.5 %convolution_add_fusion = f32[128,3072]{1,0:T(8,128)S(1)} fusion(bf16[768,3072]{1,0:T(8,128)(2,1)} %bitcast.88, f32[3072]{0:T(1024)S(1)} %reshape.354, f32[128,768]{1,0:T(8,128)S(1)} %get-tuple-element.67, f32[768]{0:T(1024)S(1)} %reshape.353, f32[768]{0:T(1024)S(1)} %reshape.352, f32[128]{0:T(128)S(1)} %add_rsqrt_fusion, f32[128]{0:T(128)S(1)} %broadcast_multiply_fusion.4), kind=kOutput, calls=%fused_computation.4 | convolution fusion | flops 604864512 | bytes 6704128 | tf_op jit(solution)/shard_map/dot_general | solution.py:518
  93.7 4.2 %fusion.9 = bf16[128,768]{1,0:T(8,128)(2,1)} fusion(f32[128,768]{1,0:T(8,128)S(1)} %get-tuple-element.67, bf16[3072,768]{1,0:T(8,128)(2,1)} %bitcast.128, f32[768]{0:T(1024)S(1)} %reshape.355, f32[128,3072]{1,0:T(8,128)S(1)} %convolution_add_fusion), kind=kOutput, calls=%fused_computation.24 | convolution fusion | flops 607813632 | bytes 6884352 | tf_op jit(solution)/shard_map/dot_general | solution.py:525
  98.0 2.5 convert_reduce_fusion
  100.5 2.3 multiply_reduce_fusion.1
  102.9 0.8 convert_reduce_fusion.3
  103.7 1.2 convolution_convert_fusion.5
  104.9 1.7 copy.65
  106.7 1.4 reshape.341
  108.0 1.4 reshape.342
  109.4 1.4 reshape.344
  110.7 1.4 reshape.343
  112.1 1.5 reshape.345
  113.6 2.6 %convert_reduce_fusion.4 = (f32[12,64]{1,0:T(8,128)}, bf16[12,64,128]{2,1,0:T(8,128)(2,1)}) fusion(bf16[128,12,64]{0,2,1:T(8,128)(2,1)} %bitcast.100, f32[12,128,128]{1,2,0:T(8,128)S(1)} %get-tuple-element.65, f32[12,128]{1,0:T(8,128)} %log_add_fusion), kind=kOutput, calls=%fused_computation.63 | convolution fusion | flops 25853184 | bytes 1188864 | tf_op jit(solution)/shard_map/hqk,qhd->khd/dot_general | solution.py:551
  116.2 1.4 reshape.340
  117.5 1.4 multiply_reduce_fusion
  119.6 0.9 convert_reduce_fusion.5
  121.0 1.9 fusion.27
  122.9 0.9 fusion.26
  123.8 0.8 reshape.339
  126.1 1.8 concatenate.11
  128.0 1.6 convolution_convert_fusion.3
  129.6 2.2 convolution_convert_fusion.2
  131.9 3.8 %convolution_convert_fusion = bf16[3072,768]{1,0:T(8,128)(2,1)} fusion(bf16[128,768]{1,0:T(8,128)(2,1)S(1)} %copy-done.12, f32[128]{0:T(128)S(1)} %copy-done.27, f32[128,3072]{1,0:T(8,128)S(1)} %convolution_add_fusion), kind=kOutput, calls=%fused_computation | convolution fusion | flops 610172928 | bytes 6488576 | tf_op jit(solution)/shard_map/dot_general | solution.py:35
  135.7 3.7 %convolution_convert_fusion.1 = bf16[768,3072]{1,0:T(8,128)(2,1)} fusion(bf16[128,3072]{1,0:T(8,128)(2,1)S(1)} %copy-done.4, f32[128,768]{1,0:T(8,128)S(1)} %get-tuple-element.67, f32[768]{0:T(1024)S(1)} %reshape.353, f32[768]{0:T(1024)S(1)} %reshape.352, f32[128]{0:T(128)S(1)} %copy-done.18, f32[128]{0:T(128)S(1)} %copy-done.16), kind=kOutput, calls=%fused_computation.1 | convolution fusion | flops 606830592 | bytes 5905408 | tf_op jit(solution)/shard_map/dot_general | solution.py:35
  139.4 113.6 %shard_map.290 = (f32[24,2304]{1,0:T(8,128)S(1)}, f32[24,768]{1,0:T(8,128)S(1)}, f32[24,3072]{1,0:T(8,128)S(1)}, f32[96,768]{1,0:T(8,128)S(1)}, f32[16,128]{1,0:T(8,128)S(1)}) custom-call(bf16[32,24,2304]{2,1,0:T(8,128)(2,1)S(1)} %bitcast.84, bf16[32,24,768]{2,1,0:T(8,128)(2,1)S(1)} %bitcast.85, bf16[32,24,3072]{2,1,0:T(8,128)(2,1)} %bitcast.87, ...), custom_call_target="tpu_custom_call" | custom-call | tf_op jit(solution)/shard_map/pallas_call | solution.py:348
  (115 shorter events, 13.9 us)
Async XLA Ops:
  0.6 83.1 %copy-start = (bf16[128,768]{1,0:T(8,128)(2,1)S(1)}, bf16[128,768]{1,0:T(8,128)(2,1)}, u32[]{:S(2)}) copy-start(bf16[128,768]{1,0:T(8,128)(2,1)} %param.18) | copy-start | bytes 589828
  3.1 83.3 %copy-start.19 = (f32[128]{0:T(128)}, f32[128]{0:T(128)S(1)}, u32[]{:S(2)}) copy-start(f32[128]{0:T(128)S(1)} %broadcast_multiply_fusion.5) | copy-start | bytes 1540
  4.2 82.2 %copy-start.22 = (f32[128]{0:T(128)}, f32[128]{0:T(128)S(1)}, u32[]{:S(2)}) copy-start(f32[128]{0:T(128)S(1)} %add_rsqrt_fusion.1) | copy-start | bytes 1540
  5.0 92.9 %copy-start.25 = (f32[128]{0:T(128)}, f32[128]{0:T(128)S(1)}, u32[]{:S(2)}) copy-start(f32[128]{0:T(128)S(1)} %compare_convert_fusion) | copy-start | bytes 1540
  86.7 1.7 copy-start.5
  87.0 1.4 copy-start.13
  88.1 1.3 copy-start.1
  88.4 1.7 copy-start.10
  89.5 8.5 %slice-start.2 = ((s8[4718592]{0:T(1024)(128)(4,1)}), s8[4194304]{0:T(1024)(128)(4,1)S(1)}, s32[]{:S(2)}) async-start(s8[4718592]{0:T(1024)(128)(4,1)} %bitcast.129), calls=%async_computation.2 | async-start | bytes 8388608
  89.9 12.9 %copy-start.15 = (f32[128]{0:T(128)}, f32[128]{0:T(128)S(1)}, u32[]{:S(2)}) copy-start(f32[128]{0:T(128)S(1)} %broadcast_multiply_fusion.4) | copy-start | bytes 1540
  90.2 12.7 %copy-start.17 = (f32[128]{0:T(128)}, f32[128]{0:T(128)S(1)}, u32[]{:S(2)}) copy-start(f32[128]{0:T(128)S(1)} %add_rsqrt_fusion) | copy-start | bytes 1540
  90.2 7.8 %slice-start.3 = ((s8[4718592]{0:T(1024)(128)(4,1)}), s8[524288]{0:T(1024)(128)(4,1)S(1)}, s32[]{:S(2)}) async-start(s8[4718592]{0:T(1024)(128)(4,1)} %bitcast.129), calls=%async_computation.3 | async-start | bytes 1048576
  93.7 4.3 %copy-start.11 = (bf16[128,768]{1,0:T(8,128)(2,1)S(1)}, bf16[128,768]{1,0:T(8,128)(2,1)}, u32[]{:S(2)}) copy-start(bf16[128,768]{1,0:T(8,128)(2,1)} %param.19) | copy-start | bytes 589828
  93.7 6.8 %slice-start = ((s8[4718592]{0:T(1024)(128)(4,1)}), s8[4194304]{0:T(1024)(128)(4,1)S(1)}, s32[]{:S(2)}) async-start(s8[4718592]{0:T(1024)(128)(4,1)} %bitcast.89), calls=%async_computation | async-start | bytes 8388608
  98.0 2.5 slice-start.1
  100.5 2.3 copy-start.3
  100.5 2.4 copy-start.26
  117.5 1.4 copy-start.14
  117.5 1.6 copy-start.6
  117.5 3.0 %copy-start.7 = (bf16[12,64,128]{2,1,0:T(8,128)(2,1)S(1)}, bf16[12,64,128]{2,1,0:T(8,128)(2,1)}, u32[]{:S(2)}) copy-start(bf16[12,64,128]{2,1,0:T(8,128)(2,1)} %get-tuple-element.75) | copy-start | bytes 589828
  119.0 2.0 copy-start.2
  119.0 2.0 copy-start.20
  119.0 2.0 copy-start.23
  120.5 2.4 copy-start.9
  123.8 5.8 %copy-start.8 = (bf16[12,64,128]{2,1,0:T(8,128)(2,1)S(1)}, bf16[12,64,128]{2,1,0:T(8,128)(2,1)}, u32[]{:S(2)}) copy-start(bf16[12,64,128]{2,1,0:T(8,128)(2,1)} %get-tuple-element.75) | copy-start | bytes 589828
  123.8 5.8 %copy-start.21 = (f32[128]{0:T(128)S(1)}, f32[128]{0:T(128)}, u32[]{:S(2)}) copy-start(f32[128]{0:T(128)} %copy-done.19) | copy-start | bytes 1540
  123.8 5.8 %copy-start.24 = (f32[128]{0:T(128)S(1)}, f32[128]{0:T(128)}, u32[]{:S(2)}) copy-start(f32[128]{0:T(128)} %copy-done.22) | copy-start | bytes 1540
  129.6 2.2 copy-start.12
  129.6 2.2 copy-start.27
  131.9 3.9 %copy-start.4 = (bf16[128,3072]{1,0:T(8,128)(2,1)S(1)}, bf16[128,3072]{1,0:T(8,128)(2,1)}, u32[]{:S(2)}) copy-start(bf16[128,3072]{1,0:T(8,128)(2,1)} %copy-done.3) | copy-start | bytes 2359300
  131.9 3.9 %copy-start.16 = (f32[128]{0:T(128)S(1)}, f32[128]{0:T(128)}, u32[]{:S(2)}) copy-start(f32[128]{0:T(128)} %copy-done.15) | copy-start | bytes 1540
  131.9 3.8 %copy-start.18 = (f32[128]{0:T(128)S(1)}, f32[128]{0:T(128)}, u32[]{:S(2)}) copy-start(f32[128]{0:T(128)} %copy-done.17) | copy-start | bytes 1540

commit v2 on v1

--- a/solution.py
+++ b/solution.py
@@ -140,13 +140,15 @@
     ]
     home = (0, 0, 0, 0)
     pieces = range(len(PIECES))
-    for step in (3, 1, 2):
+    for n in pieces:
+        order = PIECES[n][3]
+        send(n, home, (1, 0, 0, 0)).start()
+        send(n, home, mask_of(order, 0, 1, 0, 0)).start()
+        send(n, home, mask_of(order, 0, 0, 1, 0)).start()
+    for step in (2, 3):
         for n in pieces:
             send(n, home, (step, 0, 0, 0)).start()
     for n in pieces:
-        order = PIECES[n][3]
-        send(n, home, mask_of(order, 0, 1, 0, 0)).start()
-        send(n, home, mask_of(order, 0, 0, 1, 0)).start()
         send(n, home, (0, 0, 0, 1)).start()
     for copy in own:
         copy.start()
@@ -168,23 +170,27 @@
             send(n, held, mask_of(order, 0, 0, 1, 0)).start()
             send(n, held, (0, 0, 0, 1)).start()
 
-    def third(k):
-        for n in pieces:
-            held = mask_of(PIECES[n][3], k % 4, k // 4, 1, 0)
-            arrived(n, held).wait_recv()
-            send(n, held, (0, 0, 0, 1)).start()
+    def third(zm):
+        for bit in (0, 1):
+            for n in pieces:
+                held = mask_of(PIECES[n][3], zm, bit, 1, 0)
+                arrived(n, held).wait_recv()
+                send(n, held, (0, 0, 0, 1)).start()
 
     @pl.loop(1, 4)
     def _(zm):
         along(zm)
-
-    @pl.loop(0, 4)
+        second(zm - 1)
+
+        @pl.when(zm >= 2)
+        def _():
+            third(zm - 2)
+
+    second(3)
+
+    @pl.loop(2, 4)
     def _(zm):
-        second(zm)
-
-    @pl.loop(0, 8)
-    def _(k):
-        third(k)
+        third(zm)
 
     @pl.loop(0, 16)
     def _(k):
@@ -273,49 +279,37 @@
                 value = value + term[:, begin : begin + width].astype(jnp.float32)
             result[:, begin : begin + width] = value.astype(result.dtype)
 
-    def loads(third, k):
-        for n in pieces:
-            mask = mask_of(PIECES[n][3], k % 4, 1 - k // 4, third, 0)
-            load(n, mask).start()
-
-    def sends(third, k):
-        for n in pieces:
-            mask = mask_of(PIECES[n][3], k % 4, 1 - k // 4, third, 0)
-            across(n, mask).start()
-
-    @pl.loop(0, 8)
+    def begin(zm, action):
+        for third, second in ((1, 1), (1, 0), (0, 1), (0, 0)):
+            for n in pieces:
+                action(n, mask_of(PIECES[n][3], zm, second, third, 0)).start()
+
+    @pl.loop(0, 4)
     def _(k):
-        loads(1, k)
+        begin(3 - k, load)
 
     greet(device)
 
-    @pl.loop(0, 8)
+    @pl.loop(0, 4)
     def _(k):
-        sends(1, k)
-
-    @pl.loop(0, 8)
-    def _(k):
-        loads(0, k)
-        sends(0, k)
-
-    @pl.loop(0, 8)
-    def _(k):
-        for n in pieces:
-            order = PIECES[n][3]
-            mask = mask_of(order, k % 4, 1 - k // 4, 1, 0)
-            total(n, mask, [mask[:3] + (1,)])
-            onward(n, mask, mask_of(order, 0, 0, 1, 0)).start()
-
-    @pl.loop(0, 4)
-    def _(zm):
+        begin(3 - k, across)
+
+    def first_sums(zm):
+        for second in (1, 0):
+            for n in pieces:
+                order = PIECES[n][3]
+                mask = mask_of(order, zm, second, 1, 0)
+                total(n, mask, [mask[:3] + (1,)])
+                onward(n, mask, mask_of(order, 0, 0, 1, 0)).start()
+
+    def second_sums(zm):
         for n in pieces:
             order = PIECES[n][3]
             mask = mask_of(order, zm, 1, 0, 0)
             total(n, mask, [mask[:3] + (1,), mask_of(order, zm, 1, 1, 0)])
             onward(n, mask, mask_of(order, 0, 1, 0, 0)).start()
 
-    @pl.loop(1, 4)
-    def _(zm):
+    def third_sums(zm):
         for n in pieces:
             order = PIECES[n][3]
             mask = (zm, 0, 0, 0)
@@ -325,6 +319,20 @@
                 [(zm, 0, 0, 1), mask_of(order, zm, 0, 1, 0), mask_of(order, zm, 1, 0, 0)],
             )
             onward(n, mask, mask).start()
+
+    @pl.loop(0, 6)
+    def _(k):
+        @pl.when(k < 4)
+        def _():
+            first_sums(3 - k)
+
+        @pl.when((k >= 1) & (k < 5))
+        def _():
+            second_sums(4 - k)
+
+        @pl.when((k >= 2) & (k < 5))
+        def _():
+            third_sums(5 - k)
 
     for n in pieces:
         order = PIECES[n][3]

time: 258 us -> 229 us (0.89)
  the two profiles are of different devices: /device:TPU:9 before, /device:TPU:0 now
where the time goes in v2:
time: 229 us; the launch traced here: 228 us
  Pallas kernels  159 us (69%)
  matrix products  36 us (16%)
  local copies, waits for them, and re-layouts  24.1 us (11%)
  other arithmetic  7.65 us (3%)
    pallas_call x1, Pallas kernels, scatter_all(): pl.pallas_call(scatter_kernel, out_shape=[jax.ShapeDtypeStruct(piece.shap...  84.1 us
    pallas_call x1, Pallas kernels, gather_all(): pl.pallas_call(gather_kernel, out_shape=[jax.ShapeDtypeStruct((devices_al...  74.6 us
    dot_general x4, matrix products, outer_sum(): lax.dot_general(left, right, (((0,), (0,)), ((), ())), preferred_element_...  11.3 us
    reshape x9, local copies, waits for them, and re-layouts, scatter_grads(): table = [v.reshape(devices_all, -1, rows) for v in vectors]  10.6 us
    dot_general x4, matrix products, through(): lax.dot_general(left, weight, (((1,), (1,)), ((), ())), preferred_element...  8.01 us

profile of v2, /device:TPU:0, one launch (start us, length us, event | category | flops | bytes accessed | tf_op | source)
XLA Modules:
  0.0 227.7 jit_solution(1446988065404880701)
XLA Ops:
  2.0 1.0 convert_reduce_fusion.1
  3.1 1.1 fusion.28
  5.8 0.8 concatenate.9
  7.3 74.6 %shard_map.289 = (bf16[32,24,2304]{2,1,0:T(8,128)(2,1)}, bf16[32,24,768]{2,1,0:T(8,128)(2,1)}, bf16[32,24,3072]{2,1,0:T(8,128)(2,1)}, bf16[32,96,768]{2,1,0:T(8,128)(2,1)}, bf16[32,16,128]{2,1,0:T(8,128)(2,1)}) custom-call(bf16[24,2304]{1,0:T(8,128)(2,1)} %refs_0_.1, bf16[24,768]{1,0:T(8,128)(2,1)} %refs_1_.1, bf16[24,3072]{1,0:T(8,128)(2,1)} %refs_2_.1, ...), custom_call_target="tpu_custom_call" | custom-call | tf_op jit(solution)/shard_map/pallas_call | solution.py:210
  81.9 0.9 slice_bitcast_fusion
  84.1 2.7 %fusion.53 = f32[128,2304]{1,0:T(8,128)S(1)} fusion(bf16[768,2304]{1,0:T(8,128)(2,1)} %bitcast.94, bf16[128,768]{1,0:T(8,128)(2,1)S(1)} %copy-done, f32[768]{0:T(1024)S(1)} %reshape.348, f32[768]{0:T(1024)S(1)} %reshape.347, f32[128]{0:T(128)S(1)} %add_rsqrt_fusion.1, f32[128]{0:T(128)S(1)} %broadcast_multiply_fusion.5), kind=kOutput, calls=%fused_computation.126 | convolution fusion | flops 453574656 | bytes 4922368 | tf_op jit(solution)/shard_map/dot_general | solution.py:491
  88.7 1.0 copy-done.1
  90.5 3.5 %convolution_add_fusion = f32[128,3072]{1,0:T(8,128)S(1)} fusion(bf16[768,3072]{1,0:T(8,128)(2,1)} %bitcast.88, f32[3072]{0:T(1024)S(1)} %reshape.354, f32[128,768]{1,0:T(8,128)S(1)} %get-tuple-element.67, f32[768]{0:T(1024)S(1)} %reshape.353, f32[768]{0:T(1024)S(1)} %reshape.352, f32[128]{0:T(128)S(1)} %add_rsqrt_fusion, f32[128]{0:T(128)S(1)} %broadcast_multiply_fusion.4), kind=kOutput, calls=%fused_computation.4 | convolution fusion | flops 604864512 | bytes 6704128 | tf_op jit(solution)/shard_map/dot_general | solution.py:526
  94.1 4.2 %fusion.9 = bf16[128,768]{1,0:T(8,128)(2,1)} fusion(f32[128,768]{1,0:T(8,128)S(1)} %get-tuple-element.67, bf16[3072,768]{1,0:T(8,128)(2,1)} %bitcast.128, f32[768]{0:T(1024)S(1)} %reshape.355, f32[128,3072]{1,0:T(8,128)S(1)} %convolution_add_fusion), kind=kOutput, calls=%fused_computation.24 | convolution fusion | flops 607813632 | bytes 6884352 | tf_op jit(solution)/shard_map/dot_general | solution.py:533
  98.3 2.5 %convert_reduce_fusion = (f32[3072]{0:T(1024)}, bf16[128,3072]{1,0:T(8,128)(2,1)S(1)}) fusion(f32[128,3072]{1,0:T(8,128)S(1)} %convolution_add_fusion, bf16[3072,768]{1,0:T(8,128)(2,1)S(1)} %bitcast.131, bf16[128,768]{1,0:T(8,128)(2,1)S(1)} %copy-done.11, f32[128]{0:T(128)S(1)} %compare_convert_fusion), kind=kOutput, calls=%fused_computation.13 | convolution fusion | flops 612529152 | bytes 7287296 | tf_op jit(solution)/shard_map/dot_general | solution.py:41
  100.8 2.3 %multiply_reduce_fusion.1 = (f32[768]{0:T(1024)}, f32[128]{0:T(128)S(1)}, f32[128]{0:T(128)S(1)}, f32[768]{0:T(1024)}, f32[128,768]{1,0:T(8,128)S(1)}) fusion(f32[128,768]{1,0:T(8,128)S(1)} %get-tuple-element.67, f32[128]{0:T(128)S(1)} %add_rsqrt_fusion, f32[128]{0:T(128)S(1)} %broadcast_multiply_fusion.4, f32[768]{0:T(1024)S(1)} %reshape.352, ...), kind=kOutput, calls=%fused_computation.61 | convolution fusion | flops 604862720 | bytes 6302720 | tf_op jit(solution)/shard_map/dot_general | solution.py:41
  103.2 0.8 convert_reduce_fusion.3
  104.0 1.2 convolution_convert_fusion.5
  105.2 1.7 copy.65
  107.0 1.4 reshape.341
  108.3 1.4 reshape.342
  109.7 1.4 reshape.344
  111.1 1.4 reshape.343
  112.4 1.5 reshape.345
  113.9 2.6 %convert_reduce_fusion.4 = (f32[12,64]{1,0:T(8,128)}, bf16[12,64,128]{2,1,0:T(8,128)(2,1)}) fusion(bf16[128,12,64]{0,2,1:T(8,128)(2,1)} %bitcast.100, f32[12,128,128]{1,2,0:T(8,128)S(1)} %get-tuple-element.65, f32[12,128]{1,0:T(8,128)} %log_add_fusion), kind=kOutput, calls=%fused_computation.63 | convolution fusion | flops 25853184 | bytes 1188864 | tf_op jit(solution)/shard_map/hqk,qhd->khd/dot_general | solution.py:559
  116.5 1.4 reshape.340
  117.9 1.4 multiply_reduce_fusion
  119.9 0.9 convert_reduce_fusion.5
  121.3 2.0 fusion.27
  123.3 0.9 fusion.26
  124.1 0.8 reshape.339
  126.5 1.8 concatenate.11
  128.3 1.6 convolution_convert_fusion.3
  130.0 2.2 convolution_convert_fusion.2
  132.2 3.8 %convolution_convert_fusion = bf16[3072,768]{1,0:T(8,128)(2,1)} fusion(bf16[128,768]{1,0:T(8,128)(2,1)S(1)} %copy-done.12, f32[128]{0:T(128)S(1)} %copy-done.27, f32[128,3072]{1,0:T(8,128)S(1)} %convolution_add_fusion), kind=kOutput, calls=%fused_computation | convolution fusion | flops 610172928 | bytes 6488576 | tf_op jit(solution)/shard_map/dot_general | solution.py:35
  136.1 3.7 %convolution_convert_fusion.1 = bf16[768,3072]{1,0:T(8,128)(2,1)} fusion(bf16[128,3072]{1,0:T(8,128)(2,1)S(1)} %copy-done.4, f32[128,768]{1,0:T(8,128)S(1)} %get-tuple-element.67, f32[768]{0:T(1024)S(1)} %reshape.353, f32[768]{0:T(1024)S(1)} %reshape.352, f32[128]{0:T(128)S(1)} %copy-done.18, f32[128]{0:T(128)S(1)} %copy-done.16), kind=kOutput, calls=%fused_computation.1 | convolution fusion | flops 606830592 | bytes 5905408 | tf_op jit(solution)/shard_map/dot_general | solution.py:35
  139.7 84.1 %shard_map.290 = (f32[24,2304]{1,0:T(8,128)S(1)}, f32[24,768]{1,0:T(8,128)S(1)}, f32[24,3072]{1,0:T(8,128)S(1)}, f32[96,768]{1,0:T(8,128)S(1)}, f32[16,128]{1,0:T(8,128)S(1)}) custom-call(bf16[32,24,2304]{2,1,0:T(8,128)(2,1)S(1)} %bitcast.84, bf16[32,24,768]{2,1,0:T(8,128)(2,1)S(1)} %bitcast.85, bf16[32,24,3072]{2,1,0:T(8,128)(2,1)} %bitcast.87, ...), custom_call_target="tpu_custom_call" | custom-call | tf_op jit(solution)/shard_map/pallas_call | solution.py:356
  (115 shorter events, 13.8 us)
Async XLA Ops:
  0.6 83.4 %copy-start = (bf16[128,768]{1,0:T(8,128)(2,1)S(1)}, bf16[128,768]{1,0:T(8,128)(2,1)}, u32[]{:S(2)}) copy-start(bf16[128,768]{1,0:T(8,128)(2,1)} %param.18) | copy-start | bytes 589828
  3.1 83.7 %copy-start.19 = (f32[128]{0:T(128)}, f32[128]{0:T(128)S(1)}, u32[]{:S(2)}) copy-start(f32[128]{0:T(128)S(1)} %broadcast_multiply_fusion.5) | copy-start | bytes 1540
  4.2 82.5 %copy-start.22 = (f32[128]{0:T(128)}, f32[128]{0:T(128)S(1)}, u32[]{:S(2)}) copy-start(f32[128]{0:T(128)S(1)} %add_rsqrt_fusion.1) | copy-start | bytes 1540
  5.0 93.2 %copy-start.25 = (f32[128]{0:T(128)}, f32[128]{0:T(128)S(1)}, u32[]{:S(2)}) copy-start(f32[128]{0:T(128)S(1)} %compare_convert_fusion) | copy-start | bytes 1540
  87.0 1.7 copy-start.5
  87.4 1.4 copy-start.13
  88.5 1.3 copy-start.1
  88.7 1.7 copy-start.10
  89.8 8.5 %slice-start.2 = ((s8[4718592]{0:T(1024)(128)(4,1)}), s8[4194304]{0:T(1024)(128)(4,1)S(1)}, s32[]{:S(2)}) async-start(s8[4718592]{0:T(1024)(128)(4,1)} %bitcast.129), calls=%async_computation.2 | async-start | bytes 8388608
  90.3 12.9 %copy-start.15 = (f32[128]{0:T(128)}, f32[128]{0:T(128)S(1)}, u32[]{:S(2)}) copy-start(f32[128]{0:T(128)S(1)} %broadcast_multiply_fusion.4) | copy-start | bytes 1540
  90.5 12.7 %copy-start.17 = (f32[128]{0:T(128)}, f32[128]{0:T(128)S(1)}, u32[]{:S(2)}) copy-start(f32[128]{0:T(128)S(1)} %add_rsqrt_fusion) | copy-start | bytes 1540
  90.5 7.8 %slice-start.3 = ((s8[4718592]{0:T(1024)(128)(4,1)}), s8[524288]{0:T(1024)(128)(4,1)S(1)}, s32[]{:S(2)}) async-start(s8[4718592]{0:T(1024)(128)(4,1)} %bitcast.129), calls=%async_computation.3 | async-start | bytes 1048576
  94.0 4.3 %copy-start.11 = (bf16[128,768]{1,0:T(8,128)(2,1)S(1)}, bf16[128,768]{1,0:T(8,128)(2,1)}, u32[]{:S(2)}) copy-start(bf16[128,768]{1,0:T(8,128)(2,1)} %param.19) | copy-start | bytes 589828
  94.0 6.8 %slice-start = ((s8[4718592]{0:T(1024)(128)(4,1)}), s8[4194304]{0:T(1024)(128)(4,1)S(1)}, s32[]{:S(2)}) async-start(s8[4718592]{0:T(1024)(128)(4,1)} %bitcast.89), calls=%async_computation | async-start | bytes 8388608
  98.3 2.5 %slice-start.1 = ((s8[4718592]{0:T(1024)(128)(4,1)}), s8[524288]{0:T(1024)(128)(4,1)S(1)}, s32[]{:S(2)}) async-start(s8[4718592]{0:T(1024)(128)(4,1)} %bitcast.89), calls=%async_computation.1 | async-start | bytes 1048576
  100.8 2.3 %copy-start.3 = (bf16[128,3072]{1,0:T(8,128)(2,1)}, bf16[128,3072]{1,0:T(8,128)(2,1)S(1)}, u32[]{:S(2)}) copy-start(bf16[128,3072]{1,0:T(8,128)(2,1)S(1)} %get-tuple-element.77) | copy-start | bytes 2359300
  100.8 2.4 %copy-start.26 = (f32[128]{0:T(128)S(1)}, f32[128]{0:T(128)}, u32[]{:S(2)}) copy-start(f32[128]{0:T(128)} %copy-done.25) | copy-start | bytes 1540
  117.9 1.4 copy-start.14
  117.9 1.6 copy-start.6
  117.9 2.9 %copy-start.7 = (bf16[12,64,128]{2,1,0:T(8,128)(2,1)S(1)}, bf16[12,64,128]{2,1,0:T(8,128)(2,1)}, u32[]{:S(2)}) copy-start(bf16[12,64,128]{2,1,0:T(8,128)(2,1)} %get-tuple-element.75) | copy-start | bytes 589828
  119.3 2.0 copy-start.2
  119.3 2.0 copy-start.20
  119.3 2.0 copy-start.23
  120.8 2.4 %copy-start.9 = (bf16[12,64,128]{2,1,0:T(8,128)(2,1)}, bf16[12,64,128]{2,1,0:T(8,128)(2,1)S(1)}, u32[]{:S(2)}) copy-start(bf16[12,64,128]{2,1,0:T(8,128)(2,1)S(1)} %get-tuple-element.73) | copy-start | bytes 589828
  124.1 5.8 %copy-start.8 = (bf16[12,64,128]{2,1,0:T(8,128)(2,1)S(1)}, bf16[12,64,128]{2,1,0:T(8,128)(2,1)}, u32[]{:S(2)}) copy-start(bf16[12,64,128]{2,1,0:T(8,128)(2,1)} %get-tuple-element.75) | copy-start | bytes 589828
  124.1 5.8 %copy-start.21 = (f32[128]{0:T(128)S(1)}, f32[128]{0:T(128)}, u32[]{:S(2)}) copy-start(f32[128]{0:T(128)} %copy-done.19) | copy-start | bytes 1540
  124.1 5.8 %copy-start.24 = (f32[128]{0:T(128)S(1)}, f32[128]{0:T(128)}, u32[]{:S(2)}) copy-start(f32[128]{0:T(128)} %copy-done.22) | copy-start | bytes 1540
  129.9 2.2 copy-start.12
  130.0 2.2 copy-start.27
  132.2 3.9 %copy-start.4 = (bf16[128,3072]{1,0:T(8,128)(2,1)S(1)}, bf16[128,3072]{1,0:T(8,128)(2,1)}, u32[]{:S(2)}) copy-start(bf16[128,3072]{1,0:T(8,128)(2,1)} %copy-done.3) | copy-start | bytes 2359300
  132.2 3.9 %copy-start.16 = (f32[128]{0:T(128)S(1)}, f32[128]{0:T(128)}, u32[]{:S(2)}) copy-start(f32[128]{0:T(128)} %copy-done.15) | copy-start | bytes 1540
  132.2 3.8 %copy-start.18 = (f32[128]{0:T(128)S(1)}, f32[128]{0:T(128)}, u32[]{:S(2)}) copy-start(f32[128]{0:T(128)} %copy-done.17) | copy-start | bytes 1540

commit v3 on v2

--- a/solution.py
+++ b/solution.py
@@ -422,6 +422,74 @@
 
 def kernels_fit(devices_all, rows):
     return devices_all == 32 and rows % 8 == 0 and rows <= LANES
+
+
+def attention_forward_kernel(q_ref, k_ref, v_ref, down_ref, along_ref, out_ref):
+    slots, width = q_ref.shape
+    rows = lax.broadcasted_iota(jnp.int32, (slots, slots), 0)
+    columns = lax.broadcasted_iota(jnp.int32, (slots, slots), 1)
+    allowed = (down_ref[...] == along_ref[...]) & (columns <= rows)
+    for begin in range(0, width, 2 * HD):
+        q2, k2, v2 = (ref[:, begin : begin + 2 * HD] for ref in (q_ref, k_ref, v_ref))
+        parts = []
+        for half in (0, HD):
+            q, k, v = (piece[:, half : half + HD] for piece in (q2, k2, v2))
+            masked = jnp.where(allowed, through(q, k) * 0.125, -1e30)
+            top = jnp.max(masked, axis=-1, keepdims=True)
+            expo = jnp.exp(masked - top)
+            probs = expo / jnp.sum(expo, axis=-1, keepdims=True)
+            parts.append(
+                jnp.dot(probs.astype(jnp.bfloat16), v, preferred_element_type=jnp.float32)
+            )
+        out_ref[:, begin : begin + 2 * HD] = jnp.concatenate(parts, axis=1).astype(jnp.bfloat16)
+
+
+def attention_forward(query, keys, values, labels):
+    return pl.pallas_call(
+        attention_forward_kernel,
+        out_shape=jax.ShapeDtypeStruct(query.shape, jnp.bfloat16),
+    )(query, keys, values, labels[:, None], labels[None, :])
+
+
+def attention_backward_kernel(q_ref, k_ref, v_ref, go_ref, down_ref, along_ref, out_ref):
+    slots, width = q_ref.shape
+    rows = lax.broadcasted_iota(jnp.int32, (slots, slots), 0)
+    columns = lax.broadcasted_iota(jnp.int32, (slots, slots), 1)
+    allowed = (down_ref[...] == along_ref[...]) & (columns <= rows)
+
+    def plain(left, right):
+        return jnp.dot(left, right, preferred_element_type=jnp.float32)
+
+    for begin in range(0, width, 2 * HD):
+        q2, k2, v2, go2 = (
+            ref[:, begin : begin + 2 * HD] for ref in (q_ref, k_ref, v_ref, go_ref)
+        )
+        parts = []
+        for half in (0, HD):
+            q, k, v, go = (piece[:, half : half + HD] for piece in (q2, k2, v2, go2))
+            masked = jnp.where(allowed, through(q, k) * 0.125, -1e30)
+            top = jnp.max(masked, axis=-1, keepdims=True)
+            total = jnp.sum(jnp.exp(masked - top), axis=-1, keepdims=True)
+            probs = jnp.exp(masked - (top + jnp.log(total)))
+            grad_probs = through(go, v)
+            grad_v = outer_sum(probs.astype(jnp.bfloat16), go)
+            inner = jnp.sum(grad_probs * probs, axis=-1, keepdims=True)
+            grad_scores = (probs * (grad_probs - inner)).astype(jnp.bfloat16)
+            parts.append(
+                (plain(grad_scores, k) * 0.125, outer_sum(grad_scores, q) * 0.125, grad_v)
+            )
+        for which in range(3):
+            both = jnp.concatenate([parts[0][which], parts[1][which]], axis=1)
+            at = which * width + begin
+            out_ref[:, at : at + 2 * HD] = both.astype(jnp.bfloat16)
+
+
+def attention_backward(query, keys, values, grad_mixed, labels):
+    slots, width = query.shape
+    return pl.pallas_call(
+        attention_backward_kernel,
+        out_shape=jax.ShapeDtypeStruct((slots, 3 * width), jnp.bfloat16),
+    )(query, keys, values, grad_mixed, labels[:, None], labels[None, :])
 
 
 def body(
@@ -481,7 +549,6 @@
     )
     numbers = jnp.arange(lengths.shape[0], dtype=jnp.int32)[:, None] + 1
     labels = jnp.sum(jnp.where(inside, numbers, 0), axis=0) - 1
-    allowed = (labels[:, None] == labels[None, :]) & (slots[None, :] <= slots[:, None])
     valid = (labels >= 0).astype(jnp.float32)
     inputs = tokens.astype(jnp.float32)
     first_out, normal_one, inv_one = norm_forward(
@@ -489,31 +556,10 @@
     )
     normed = first_out.astype(jnp.bfloat16)
     joined = jnp.dot(normed, w_joined, preferred_element_type=jnp.float32)
-    query = (
-        (joined[:, :width] + bias_query.astype(jnp.float32))
-        .astype(jnp.bfloat16)
-        .reshape(slot_count, H, HD)
-    )
-    keys = joined[:, width : 2 * width].astype(jnp.bfloat16).reshape(slot_count, H, HD)
-    values = (
-        (joined[:, 2 * width :] + bias_value.astype(jnp.float32))
-        .astype(jnp.bfloat16)
-        .reshape(slot_count, H, HD)
-    )
-    scores = jnp.einsum("qhd,khd->hqk", query, keys, preferred_element_type=jnp.float32) * 0.125
-    masked = jnp.where(allowed[None], scores, -1e30)
-    row_top = jnp.max(masked, axis=-1, keepdims=True)
-    expo = jnp.exp(masked - row_top)
-    row_total = jnp.sum(expo, axis=-1, keepdims=True)
-    probs = expo / row_total
-    log_total = row_top + jnp.log(row_total)
-    mixed = (
-        jnp.einsum(
-            "hqk,khd->qhd", probs.astype(jnp.bfloat16), values, preferred_element_type=jnp.float32
-        )
-        .reshape(slot_count, width)
-        .astype(jnp.bfloat16)
-    )
+    query_flat = (joined[:, :width] + bias_query.astype(jnp.float32)).astype(jnp.bfloat16)
+    keys_flat = joined[:, width : 2 * width].astype(jnp.bfloat16)
+    values_flat = (joined[:, 2 * width :] + bias_value.astype(jnp.float32)).astype(jnp.bfloat16)
+    mixed = attention_forward(query_flat, keys_flat, values_flat, labels)
     middle = (
         inputs
         + jnp.dot(mixed, w_project, preferred_element_type=jnp.float32)
@@ -552,30 +598,12 @@
     grad_branch = grad_middle.astype(jnp.bfloat16)
     grad_bias_project = column_sum(grad_branch)
     grad_w_project = outer_sum(mixed, grad_branch)
-    grad_mixed = through(grad_branch, w_project).astype(jnp.bfloat16).reshape(slot_count, H, HD)
-    again = jnp.einsum("qhd,khd->hqk", query, keys, preferred_element_type=jnp.float32) * 0.125
-    probs_again = jnp.exp(jnp.where(allowed[None], again, -1e30) - log_total)
-    grad_probs = jnp.einsum("qhd,khd->hqk", grad_mixed, values, preferred_element_type=jnp.float32)
-    grad_values = jnp.einsum(
-        "hqk,qhd->khd",
-        probs_again.astype(jnp.bfloat16),
-        grad_mixed,
-        preferred_element_type=jnp.float32,
-    )
-    row_inner = jnp.sum(grad_probs * probs_again, axis=-1, keepdims=True)
-    grad_scores = (probs_again * (grad_probs - row_inner)).astype(jnp.bfloat16)
-    grad_query = (
-        jnp.einsum("hqk,khd->qhd", grad_scores, keys, preferred_element_type=jnp.float32) * 0.125
-    )
-    grad_keys = (
-        jnp.einsum("hqk,qhd->khd", grad_scores, query, preferred_element_type=jnp.float32) * 0.125
-    )
-    grad_query = grad_query.astype(jnp.bfloat16).reshape(slot_count, width)
-    grad_keys = grad_keys.astype(jnp.bfloat16).reshape(slot_count, width)
-    grad_values = grad_values.astype(jnp.bfloat16).reshape(slot_count, width)
+    grad_mixed = through(grad_branch, w_project).astype(jnp.bfloat16)
+    grad_joined = attention_backward(query_flat, keys_flat, values_flat, grad_mixed, labels)
+    grad_query = grad_joined[:, :width]
+    grad_values = grad_joined[:, 2 * width :]
     grad_bias_query = column_sum(grad_query)
     grad_bias_value = column_sum(grad_values)
-    grad_joined = jnp.concatenate([grad_query, grad_keys, grad_values], axis=1)
     grad_w_joined = outer_sum(normed, grad_joined)
     grad_normed = through(grad_joined, w_joined)
     norm_grad_one, grad_gain_one, grad_shift_one = norm_backward(

time: 229 us -> 241 us (1.052)
  Pallas kernels: 159 us -> 172 us
  matrix products: 36 us -> 31.1 us
    pallas_call x0 -> x2, Pallas kernels: none -> 13.7 us  [the longest x1 7.58 us: attention_backward(): pl.pallas_call(attention_backward_kernel, out_shape=jax.ShapeDtypeStruct(...]
    dot_general x6 -> x0, matrix products: 5.87 us -> none  [the longest x1 2.59 us: body(): jnp.einsum('hqk,qhd->khd', probs_again.astype(jnp.bfloat16), grad_mixed,...]
where the time goes in v3:
time: 241 us; the launch traced here: 240 us
  Pallas kernels  172 us (71%)
  matrix products  31.1 us (13%)
  local copies, waits for them, and re-layouts  26.2 us (11%)
  other arithmetic  9.28 us (4%)
    pallas_call x1, Pallas kernels, scatter_all(): pl.pallas_call(scatter_kernel, out_shape=[jax.ShapeDtypeStruct(piece.shap...  84.1 us
    pallas_call x1, Pallas kernels, gather_all(): pl.pallas_call(gather_kernel, out_shape=[jax.ShapeDtypeStruct((devices_al...  74.5 us
    reshape x9, local copies, waits for them, and re-layouts, scatter_grads(): table = [v.reshape(devices_all, -1, rows) for v in vectors]  12.4 us
    dot_general x4, matrix products, through(): lax.dot_general(left, weight, (((1,), (1,)), ((), ())), preferred_element...  10.2 us
    dot_general x4, matrix products, outer_sum(): lax.dot_general(left, right, (((0,), (0,)), ((), ())), preferred_element_...  9.2 us
    pallas_call x1, Pallas kernels, attention_backward(): pl.pallas_call(attention_backward_kernel, out_shape=jax.ShapeDtypeStruct(...  7.58 us
    pallas_call x1, Pallas kernels, attention_forward(): pl.pallas_call(attention_forward_kernel, out_shape=jax.ShapeDtypeStruct(q...  6.1 us

profile of v3, /device:TPU:0, one launch (start us, length us, event | category | flops | bytes accessed | tf_op | source)
XLA Modules:
  0.0 239.9 jit_solution(11220156053795379371)
XLA Ops:
  2.0 1.0 convert_reduce_fusion.1
  3.1 1.1 fusion.23
  6.3 0.8 concatenate.6
  8.5 74.5 %shard_map.289 = (bf16[32,24,2304]{2,1,0:T(8,128)(2,1)}, bf16[32,24,768]{2,1,0:T(8,128)(2,1)}, bf16[32,24,3072]{2,1,0:T(8,128)(2,1)}, bf16[32,96,768]{2,1,0:T(8,128)(2,1)}, bf16[32,16,128]{2,1,0:T(8,128)(2,1)}) custom-call(bf16[24,2304]{1,0:T(8,128)(2,1)} %refs_0_.1, bf16[24,768]{1,0:T(8,128)(2,1)} %refs_1_.1, bf16[24,3072]{1,0:T(8,128)(2,1)} %refs_2_.1, ...), custom_call_target="tpu_custom_call" | custom-call | tf_op jit(solution)/shard_map/pallas_call | solution.py:210
  83.0 0.9 slice_bitcast_fusion
  85.1 2.7 %fusion.44 = f32[128,2304]{1,0:T(8,128)S(1)} fusion(bf16[768,2304]{1,0:T(8,128)(2,1)} %bitcast.70, bf16[128,768]{1,0:T(8,128)(2,1)S(1)} %copy-done, f32[768]{0:T(1024)S(1)} %reshape.274, f32[768]{0:T(1024)S(1)} %reshape.273, f32[128]{0:T(128)S(1)} %add_rsqrt_fusion.1, f32[128]{0:T(128)S(1)} %broadcast_multiply_fusion.5), kind=kOutput, calls=%fused_computation.105 | convolution fusion | flops 453574656 | bytes 4922368 | tf_op jit(solution)/shard_map/dot_general | solution.py:558
  89.3 6.1 %shard_map.290 = bf16[128,768]{1,0:T(8,128)(2,1)} custom-call(bf16[128,768]{1,0:T(8,128)(2,1)} %get-tuple-element.56.q_ref, bf16[128,768]{1,0:T(8,128)(2,1)} %slice.154.k_ref, bf16[128,768]{1,0:T(8,128)(2,1)} %get-tuple-element.55.v_ref, s32[128,1]{1,0:T(8,128)} %copy.45.down_ref, s32[1,128]{1,0:T(1,128)} %get-tuple-element.66.along_ref), custom_call_target="tpu_custom_call" | custom-call | tf_op jit(solution)/shard_map/pallas_call | solution.py:448
  95.4 1.5 fusion.46
  97.2 3.3 %convolution_add_fusion = f32[128,3072]{1,0:T(8,128)S(1)} fusion(bf16[768,3072]{1,0:T(8,128)(2,1)} %bitcast.66, f32[3072]{0:T(1024)S(1)} %reshape.280, f32[128,768]{1,0:T(8,128)S(1)} %get-tuple-element.69, f32[768]{0:T(1024)S(1)} %reshape.279, f32[768]{0:T(1024)S(1)} %reshape.278, f32[128]{0:T(128)S(1)} %add_rsqrt_fusion, f32[128]{0:T(128)S(1)} %broadcast_multiply_fusion.4), kind=kOutput, calls=%fused_computation.4 | convolution fusion | flops 604864512 | bytes 6704128 | tf_op jit(solution)/shard_map/dot_general | solution.py:572
  100.4 4.2 %fusion.8 = bf16[128,768]{1,0:T(8,128)(2,1)} fusion(f32[128,768]{1,0:T(8,128)S(1)} %get-tuple-element.69, bf16[3072,768]{1,0:T(8,128)(2,1)} %bitcast.90, f32[768]{0:T(1024)S(1)} %reshape.281, f32[128,3072]{1,0:T(8,128)S(1)} %convolution_add_fusion), kind=kOutput, calls=%fused_computation.20 | convolution fusion | flops 607813632 | bytes 6884352 | tf_op jit(solution)/shard_map/dot_general | solution.py:579
  104.7 2.4 %convert_reduce_fusion = (f32[3072]{0:T(1024)}, bf16[128,3072]{1,0:T(8,128)(2,1)S(1)}) fusion(f32[128,3072]{1,0:T(8,128)S(1)} %convolution_add_fusion, bf16[3072,768]{1,0:T(8,128)(2,1)S(1)} %bitcast.93, bf16[128,768]{1,0:T(8,128)(2,1)S(1)} %copy-done.7, f32[128]{0:T(128)S(1)} %compare_convert_fusion), kind=kOutput, calls=%fused_computation.13 | convolution fusion | flops 612529152 | bytes 7287296 | tf_op jit(solution)/shard_map/dot_general | solution.py:41
  107.1 2.3 multiply_reduce_fusion
  109.5 0.8 convert_reduce_fusion.3
  110.7 1.2 convolution_convert_fusion.4.go_ref
  112.0 7.6 %shard_map.291 = bf16[128,2304]{1,0:T(8,128)(2,1)} custom-call(bf16[128,768]{1,0:T(8,128)(2,1)} %get-tuple-element.56.q_ref, bf16[128,768]{1,0:T(8,128)(2,1)} %slice.154.k_ref, bf16[128,768]{1,0:T(8,128)(2,1)} %get-tuple-element.55.v_ref, bf16[128,768]{1,0:T(8,128)(2,1)} %convolution_convert_fusion.4.go_ref, s32[128,1]{1,0:T(8,128)} %copy.45.down_ref, ...), custom_call_target="tpu_custom_call" | custom-call | tf_op jit(solution)/shard_map/pallas_call | solution.py:489
  119.6 4.2 %fusion.22 = (f32[768]{0:T(1024)}, f32[128]{0:T(128)S(1)}, f32[128]{0:T(128)S(1)}, f32[768]{0:T(1024)}, f32[128,768]{1,0:T(8,128)S(1)}) fusion(bf16[128,768]{1,0:T(8,128)(2,1)S(1)} %copy-done, f32[128]{0:T(128)S(1)} %add_rsqrt_fusion.1, f32[128]{0:T(128)S(1)} %broadcast_multiply_fusion.5, f32[768]{0:T(1024)S(1)} %reshape.273, ...), kind=kOutput, calls=%fused_computation.37 | convolution fusion | flops 453966080 | bytes 4729856 | tf_op jit(solution)/shard_map/dot_general | solution.py:41
  123.8 1.6 fusion.21
  126.1 1.4 reshape.266
  127.4 1.4 reshape.267
  128.8 1.4 reshape.263
  130.2 1.4 reshape.268
  131.5 1.4 reshape.265
  132.9 1.4 reshape.270
  134.2 1.4 reshape.264
  135.6 1.4 reshape.269
  137.0 1.5 reshape.271
  138.4 3.2 %concatenate.7 = f32[32,12,24]{2,1,0:T(8,128)} concatenate(f32[32,1,24]{2,1,0:T(1,128)} %bitcast.76, f32[32,1,24]{2,1,0:T(1,128)} %bitcast.80, f32[32,1,24]{2,1,0:T(1,128)} %bitcast.78, f32[32,1,24]{2,1,0:T(1,128)} %bitcast.74, f32[32,1,24]{2,1,0:T(1,128)} %bitcast.75, f32[32,1,24]{2,1,0:T(1,128)} %bitcast.77, f32[32,1,24]{2,1,0:T(1,128)} %bitcast.81, f32[32,1,24]{2,1,0:T(1,128)} %bitcast.79, ...), dimensions={1} | concatenate | bytes 73728 | tf_op jit(solution)/shard_map/concatenate | solution.py:408
  141.6 1.0 pad.9.refs_4_
  143.2 1.2 convolution_convert_fusion.2
  144.4 3.8 %convolution_convert_fusion = bf16[3072,768]{1,0:T(8,128)(2,1)} fusion(bf16[128,768]{1,0:T(8,128)(2,1)S(1)} %copy-done.7, f32[128]{0:T(128)S(1)} %copy-done.17, f32[128,3072]{1,0:T(8,128)S(1)} %convolution_add_fusion), kind=kOutput, calls=%fused_computation | convolution fusion | flops 610172928 | bytes 6488576 | tf_op jit(solution)/shard_map/dot_general | solution.py:35
  148.2 3.7 %convolution_convert_fusion.1 = bf16[768,3072]{1,0:T(8,128)(2,1)} fusion(bf16[128,3072]{1,0:T(8,128)(2,1)S(1)} %copy-done.5, f32[128,768]{1,0:T(8,128)S(1)} %get-tuple-element.69, f32[768]{0:T(1024)S(1)} %reshape.279, f32[768]{0:T(1024)S(1)} %reshape.278, f32[128]{0:T(128)S(1)} %copy-done.11, f32[128]{0:T(128)S(1)} %copy-done.9), kind=kOutput, calls=%fused_computation.1 | convolution fusion | flops 606830592 | bytes 5905408 | tf_op jit(solution)/shard_map/dot_general | solution.py:35
  151.9 84.1 %shard_map.292 = (f32[24,2304]{1,0:T(8,128)S(1)}, f32[24,768]{1,0:T(8,128)S(1)}, f32[24,3072]{1,0:T(8,128)S(1)}, f32[96,768]{1,0:T(8,128)S(1)}, f32[16,128]{1,0:T(8,128)S(1)}) custom-call(bf16[32,24,2304]{2,1,0:T(8,128)(2,1)S(1)} %bitcast.62, bf16[32,24,768]{2,1,0:T(8,128)(2,1)S(1)} %bitcast.63, bf16[32,24,3072]{2,1,0:T(8,128)(2,1)} %bitcast.65, ...), custom_call_target="tpu_custom_call" | custom-call | tf_op jit(solution)/shard_map/pallas_call | solution.py:356
  (85 shorter events, 13.2 us)
Async XLA Ops:
  0.6 84.5 %copy-start = (bf16[128,768]{1,0:T(8,128)(2,1)S(1)}, bf16[128,768]{1,0:T(8,128)(2,1)}, u32[]{:S(2)}) copy-start(bf16[128,768]{1,0:T(8,128)(2,1)} %param.18) | copy-start | bytes 589828
  3.1 116.5 %copy-start.12 = (f32[128]{0:T(128)}, f32[128]{0:T(128)S(1)}, u32[]{:S(2)}) copy-start(f32[128]{0:T(128)S(1)} %broadcast_multiply_fusion.5) | copy-start | bytes 1540
  4.2 115.3 %copy-start.14 = (f32[128]{0:T(128)}, f32[128]{0:T(128)S(1)}, u32[]{:S(2)}) copy-start(f32[128]{0:T(128)S(1)} %add_rsqrt_fusion.1) | copy-start | bytes 1540
  5.0 104.4 %copy-start.16 = (f32[128]{0:T(128)}, f32[128]{0:T(128)S(1)}, u32[]{:S(2)}) copy-start(f32[128]{0:T(128)S(1)} %compare_convert_fusion) | copy-start | bytes 1540
  87.8 7.6 %copy-start.2 = (bf16[32,24,768]{2,1,0:T(8,128)(2,1)S(1)}, bf16[32,24,768]{2,1,0:T(8,128)(2,1)}, u32[]{:S(2)}) copy-start(bf16[32,24,768]{2,1,0:T(8,128)(2,1)} %get-tuple-element.27) | copy-start | bytes 3538948
  95.4 9.2 %slice-start.2 = ((s8[4718592]{0:T(1024)(128)(4,1)}), s8[4194304]{0:T(1024)(128)(4,1)S(1)}, s32[]{:S(2)}) async-start(s8[4718592]{0:T(1024)(128)(4,1)} %bitcast.91), calls=%async_computation.2 | async-start | bytes 8388608
  96.9 12.6 %copy-start.8 = (f32[128]{0:T(128)}, f32[128]{0:T(128)S(1)}, u32[]{:S(2)}) copy-start(f32[128]{0:T(128)S(1)} %broadcast_multiply_fusion.4) | copy-start | bytes 1540
  97.1 12.4 %copy-start.10 = (f32[128]{0:T(128)}, f32[128]{0:T(128)S(1)}, u32[]{:S(2)}) copy-start(f32[128]{0:T(128)S(1)} %add_rsqrt_fusion) | copy-start | bytes 1540
  97.1 7.5 %slice-start.3 = ((s8[4718592]{0:T(1024)(128)(4,1)}), s8[524288]{0:T(1024)(128)(4,1)S(1)}, s32[]{:S(2)}) async-start(s8[4718592]{0:T(1024)(128)(4,1)} %bitcast.91), calls=%async_computation.3 | async-start | bytes 1048576
  100.4 4.2 %copy-start.7 = (bf16[128,768]{1,0:T(8,128)(2,1)S(1)}, bf16[128,768]{1,0:T(8,128)(2,1)}, u32[]{:S(2)}) copy-start(bf16[128,768]{1,0:T(8,128)(2,1)} %param.19) | copy-start | bytes 589828
  100.4 6.7 %slice-start = ((s8[4718592]{0:T(1024)(128)(4,1)}), s8[4194304]{0:T(1024)(128)(4,1)S(1)}, s32[]{:S(2)}) async-start(s8[4718592]{0:T(1024)(128)(4,1)} %bitcast.67), calls=%async_computation | async-start | bytes 8388608
  104.7 2.5 %slice-start.1 = ((s8[4718592]{0:T(1024)(128)(4,1)}), s8[524288]{0:T(1024)(128)(4,1)S(1)}, s32[]{:S(2)}) async-start(s8[4718592]{0:T(1024)(128)(4,1)} %bitcast.67), calls=%async_computation.1 | async-start | bytes 1048576
  107.1 2.3 copy-start.4
  109.5 1.3 copy-start.3
  119.6 5.8 %copy-start.1 = (bf16[128,2304]{1,0:T(8,128)(2,1)S(1)}, bf16[128,2304]{1,0:T(8,128)(2,1)}, u32[]{:S(2)}) copy-start(bf16[128,2304]{1,0:T(8,128)(2,1)} %shard_map.291) | copy-start | bytes 1769476
  123.8 18.8 %copy-start.6 = (bf16[128,768]{1,0:T(8,128)(2,1)S(1)}, bf16[128,768]{1,0:T(8,128)(2,1)}, u32[]{:S(2)}) copy-start(bf16[128,768]{1,0:T(8,128)(2,1)} %shard_map.290) | copy-start | bytes 589828
  141.6 1.5 copy-start.13
  141.6 1.5 copy-start.15
  143.1 1.2 copy-start.17
  144.4 3.9 %copy-start.5 = (bf16[128,3072]{1,0:T(8,128)(2,1)S(1)}, bf16[128,3072]{1,0:T(8,128)(2,1)}, u32[]{:S(2)}) copy-start(bf16[128,3072]{1,0:T(8,128)(2,1)} %copy-done.4) | copy-start | bytes 2359300
  144.4 3.9 %copy-start.9 = (f32[128]{0:T(128)S(1)}, f32[128]{0:T(128)}, u32[]{:S(2)}) copy-start(f32[128]{0:T(128)} %copy-done.8) | copy-start | bytes 1540
  144.4 3.8 %copy-start.11 = (f32[128]{0:T(128)S(1)}, f32[128]{0:T(128)}, u32[]{:S(2)}) copy-start(f32[128]{0:T(128)} %copy-done.10) | copy-start | bytes 1540
